TPU v7x, 32 devices: a whole 2x2x4 slice. The times are simulated.
32 devices in a mesh: group: 2 (over y), space: 8 (over z, x), tm: 2 (over core).
Axes of the slice: x: 2, y: 2, z: 4, core: 2. Of those that a mesh axis runs over, the one named last changes fastest.
Arguments:
- snapshots: bfloat16 [2048, 8192], P(('group', 'tm'), 'space'), parts along dimension 0, may hold values from -6 to 6
- mode_columns: bfloat16 [8192, 96], P('space', 'group'), parts along dimension 1, may hold values from -0.0625 to 0.0625
- filter_taps: bfloat16 [8, 2, 257], replicated, may hold values from -1 to 1, as said below
- mode_gain: float32 [96], P('group'), parts along dimension 0, may hold values from 2 to 20
Outputs:
- band_field: bfloat16 [2048, 8192], P(('group', 'tm'), 'space'), parts along dimension 0
There are 2 independent parts, one for each index of `group`. A program takes and returns all parts, laid end to end along the dimension named above; an argument that names none is the same for every part. Nothing has to cross between parts.
Inputs may be any that keep to these rules, and one draw needn't show every extreme that they name: `filter_taps`: each frequency's taps are a tapered cosine and sine of some frequency, each tap then scaled by an independent factor between 0.5 and 1.5.
All inputs are finite; a program needn't handle non-finite values.
Results may differ from a plain program's by a relative error of at most 0.0059.
Values may be sent and summed in bfloat16 or wider, within the bound.
No kernel may reach another device: no remote copies, remote signals or barrier semaphores. Data moves between devices by JAX's collectives and lax.ppermute only.
A program may use at most 64 MiB of HBM per device.

v0:
```python
import jax
import jax.numpy as jnp
from jax import lax
from jax.sharding import PartitionSpec as P

FREQ_DEV = 1
MODES = 3
HALF = 128


def extended(cells, sides, width):
    for axis, dim in sides:
        count = lax.axis_size(axis)
        ends = count - 1
        head = lax.slice_in_dim(cells, 0, width, axis=dim)
        tail = lax.slice_in_dim(cells, cells.shape[dim] - width, cells.shape[dim], axis=dim)
        cells = jnp.concatenate(
            [
                lax.ppermute(tail, axis, [(i, (i + 1) % count) for i in range(ends)]),
                cells,
                lax.ppermute(head, axis, [((i + 1) % count, i) for i in range(ends)]),
            ],
            axis=dim,
        )
    return cells


def band_filter(coefficients, filter_taps):
    freqs = filter_taps.shape[0]
    modes = coefficients.shape[0] // (2 * freqs)
    padlen = coefficients.shape[1]
    stacked = (
        coefficients.reshape(freqs, modes, 2, padlen)
        .transpose(1, 0, 2, 3)
        .reshape(modes, freqs * 2, padlen)
    )
    cosine = filter_taps[:, 0, :]
    sine = filter_taps[:, 1, :]
    row_cos = jnp.stack([cosine, -sine], axis=1)
    row_sin = jnp.stack([sine, cosine], axis=1)
    kernel = jnp.stack([row_cos, row_sin], axis=1).reshape(freqs * 2, 2, filter_taps.shape[2])
    result = lax.conv_general_dilated(
        stacked,
        kernel,
        (1,),
        "VALID",
        feature_group_count=freqs,
        dimension_numbers=("NCH", "OIH", "NCH"),
        preferred_element_type=jnp.float32,
    )
    steps = result.shape[2]
    return (
        result.reshape(modes, freqs, 2, steps)
        .transpose(1, 0, 2, 3)
        .reshape(freqs * modes * 2, steps)
    )


def per_device(snapshots, mode_columns, filter_taps, mode_gain):
    owned_rows = 2 * MODES * FREQ_DEV
    columns = mode_columns
    owned = lax.psum_scatter(
        lax.dot_general(
            columns, snapshots, (((0,), (1,)), ((), ())), preferred_element_type=jnp.float32
        ),
        "space",
        scatter_dimension=0,
        tiled=True,
    ).astype(jnp.bfloat16)
    padded = extended(owned, (("tm", 1),), HALF)
    first = lax.axis_index("space")
    own_taps = lax.dynamic_slice_in_dim(filter_taps, first * FREQ_DEV, FREQ_DEV, 0)
    own_gain = lax.dynamic_slice_in_dim(mode_gain, first * owned_rows, owned_rows, 0)
    filtered = band_filter(padded, own_taps)
    scaled = (filtered * own_gain[:, None]).astype(jnp.bfloat16)
    empty = jnp.zeros((snapshots.shape[0], snapshots.shape[1]), jnp.float32)
    piece = lax.all_gather(scaled, "space", axis=0, tiled=True)
    columns = lax.slice_in_dim(mode_columns, 0, piece.shape[0], axis=1)
    field = empty + lax.dot_general(
        piece, columns, (((0,), (1,)), ((), ())), preferred_element_type=jnp.float32
    )
    return field.astype(jnp.bfloat16)


def solution(mesh):
    placed = (P(("group", "tm"), "space"), P("space", "group"), P(), P("group"))
    return jax.shard_map(
        per_device,
        mesh=mesh,
        in_specs=placed,
        out_specs=P(("group", "tm"), "space"),
        check_vma=False,
    )
```

profile of v0, /device:TPU:0, one launch (start us, length us, event | category | flops | bytes accessed | tf_op | source)
XLA Modules:
  0.0 94.4 jit_solution(11082052050530615029)
XLA Ops:
  0.0 0.0 copy-start
  0.0 0.0 copy-start.2
  0.0 1.2 %copy-done = bf16[512,1024]{1,0:T(8,128)(2,1)S(1)} copy-done((bf16[512,1024]{1,0:T(8,128)(2,1)S(1)}, bf16[512,1024]{1,0:T(8,128)(2,1)}, u32[]{:S(2)}) %copy-start) | copy-done | bytes 1048600
  1.2 0.0 copy-start.3
  1.2 1.3 %fusion.6 = f32[48,512]{1,0:T(8,128)S(1)} fusion(bf16[1024,48]{0,1:T(8,128)(2,1)} %param.5, bf16[512,1024]{1,0:T(8,128)(2,1)S(1)} %copy-done), kind=kOutput, calls=%fused_computation.14 | convolution fusion | flops 50331648 | bytes 1245184 | tf_op jit(solution)/shard_map/dot_general | solution.py:63
  2.6 24.3 %fusion = f32[8,512]{1,0:T(8,128)S(1)} fusion(f32[48,512]{1,0:T(8,128)S(1)} %fusion.6), kind=kCustom, calls=%all-reduce-scatter | all-reduce-scatter fusion | flops 32769 | bytes 115200
  26.9 1.9 %collective-permute-start.2 = (bf16[8,512]{1,0:T(8,128)(2,1)S(1)}, bf16[8,512]{1,0:T(8,128)(2,1)S(1)}, u32[]{:S(2)}, u32[]{:S(2)}) collective-permute-start(bf16[8,512]{1,0:T(8,128)(2,1)S(1)} %convert), channel_id=1, source_target_pairs={{0,2},{2,4},{4,6},{6,8},{8,10},{10,12},{12,14},{1,3},{3,5},{5,7},{... | collective-permute-start | bytes 24584
  28.8 1.3 %collective-permute-start.3 = (bf16[6,512]{1,0:T(8,128)(2,1)S(1)}, bf16[6,512]{1,0:T(8,128)(2,1)S(1)}, u32[]{:S(2)}, u32[]{:S(2)}) collective-permute-start(bf16[6,512]{1,0:T(8,128)(2,1)S(1)} %slice.18), channel_id=1, source_target_pairs={{0,4},{2,6},{4,8},{6,10},{8,12},{10,14},{1,5},{3,7},{5,9},{7,11},{... | collective-permute-start | bytes 18440
  30.1 0.8 fusion.4
  30.9 0.0 copy-done.2
  30.9 0.6 dynamic-slice.6
  32.2 0.0 collective-permute-done.3
  32.2 0.0 collective-permute-done.2
  32.2 0.2 concatenate.4
  32.5 1.3 %collective-permute-start = (bf16[6,128]{1,0:T(8,128)(2,1)S(1)}, bf16[6,128]{1,0:T(8,128)(2,1)S(1)}, u32[]{:S(2)}, u32[]{:S(2)}) collective-permute-start(bf16[6,128]{1,0:T(8,128)(2,1)S(1)} %get-tuple-element.8), channel_id=1, source_target_pairs={{0,1},{2,3},{4,5},{6,7},{8,9},{10,11},{12,13},{14,15},{16,17},{18,... | collective-permute-start | bytes 4616 | tf_op jit(solution)/shard_map/ppermute | solution.py:19
  33.8 1.3 %collective-permute-start.1 = (bf16[6,128]{1,0:T(8,128)(2,1)S(1)}, bf16[6,128]{1,0:T(8,128)(2,1)S(1)}, u32[]{:S(2)}, u32[]{:S(2)}) collective-permute-start(bf16[6,128]{1,0:T(8,128)(2,1)S(1)} %get-tuple-element.9), channel_id=1, source_target_pairs={{1,0},{3,2},{5,4},{7,6},{9,8},{11,10},{13,12},{15,14},{17,16},{19,... | collective-permute-start | bytes 4616 | tf_op jit(solution)/shard_map/ppermute | solution.py:21
  35.1 0.2 copy.19
  35.3 0.0 copy-done.3
  35.3 0.1 dynamic_slice.7
  35.4 0.0 collective-permute-done
  35.4 1.4 %collective-permute-done.1 = bf16[6,128]{1,0:T(8,128)(2,1)S(1)} collective-permute-done((bf16[6,128]{1,0:T(8,128)(2,1)S(1)}, bf16[6,128]{1,0:T(8,128)(2,1)S(1)}, u32[]{:S(2)}, u32[]{:S(2)}) %collective-permute-start.1) | collective-permute-done | bytes 1568 | tf_op jit(solution)/shard_map/ppermute | solution.py:21
  36.8 0.4 copy.20
  37.3 0.0 copy-start.1
  37.3 24.8 %fusion.1 = f32[3,2,512]{0,1,2:T(2,128)S(1)} fusion(bf16[3,2,768]{0,1,2:T(2,128)(2,1)S(1)} %copy.20, bf16[1,2,2,257]{2,1,3,0:T(2,128)(2,1)S(1)} %copy.19), kind=kOutput, calls=%fused_computation.1 | convolution fusion | flops 3158016 | bytes 23560 | tf_op jit(solution)/shard_map/conv_general_dilated | solution.py:42
  62.1 0.2 copy.21
  62.3 0.1 fusion.3
  62.4 30.5 %all-gather = bf16[8,6,512]{2,1,0:T(8,128)(2,1)S(1)} all-gather(bf16[1,6,512]{2,1,0:T(8,128)(2,1)S(1)} %fusion.3), channel_id=1, replica_groups=mesh['group'=2,'space'=8,'tm'=2] {'space'}, dimensions={0}, use_global_device_ids=true | all-gather | bytes 55296 | tf_op jit(solution)/shard_map/all_gather | solution.py:77
  92.9 0.0 copy-done.1
  92.9 1.4 %convolution_convert_fusion = bf16[512,1024]{1,0:T(8,128)(2,1)} fusion(bf16[48,512]{1,0:T(8,128)(2,1)S(1)} %reshape.9, bf16[1024,48]{0,1:T(8,128)(2,1)S(1)} %copy-done.1), kind=kOutput, calls=%fused_computation | convolution fusion | flops 50855936 | bytes 1196032 | tf_op jit(solution)/shard_map/dot_general | solution.py:79
  (10 shorter events, 0.1 us)
Async XLA Ops:
  0.0 1.2 %copy-start = (bf16[512,1024]{1,0:T(8,128)(2,1)S(1)}, bf16[512,1024]{1,0:T(8,128)(2,1)}, u32[]{:S(2)}) copy-start(bf16[512,1024]{1,0:T(8,128)(2,1)} %param.4) | copy-start | bytes 3145732
  0.0 30.9 %copy-start.2 = (u32[32]{0:T(128)S(1)}, u32[32]{0:T(128)}, u32[]{:S(2)}) copy-start(u32[32]{0:T(128)} %constant.16) | copy-start | bytes 388
  1.2 34.1 %copy-start.3 = (f32[48]{0:T(128)S(1)}, f32[48]{0:T(128)}, u32[]{:S(2)}) copy-start(f32[48]{0:T(128)} %param.7) | copy-start | bytes 580
  26.9 5.3 %collective-permute-start.2 = (bf16[8,512]{1,0:T(8,128)(2,1)S(1)}, bf16[8,512]{1,0:T(8,128)(2,1)S(1)}, u32[]{:S(2)}, u32[]{:S(2)}) collective-permute-start(bf16[8,512]{1,0:T(8,128)(2,1)S(1)} %convert), channel_id=1, source_target_pairs={{0,2},{2,4},{4,6},{6,8},{8,10},{10,12},{12,14},{1,3},{3,5},{5,7},{... | collective-permute-start | bytes 24584
  28.8 3.3 %collective-permute-start.3 = (bf16[6,512]{1,0:T(8,128)(2,1)S(1)}, bf16[6,512]{1,0:T(8,128)(2,1)S(1)}, u32[]{:S(2)}, u32[]{:S(2)}) collective-permute-start(bf16[6,512]{1,0:T(8,128)(2,1)S(1)} %slice.18), channel_id=1, source_target_pairs={{0,4},{2,6},{4,8},{6,10},{8,12},{10,14},{1,5},{3,7},{5,9},{7,11},{... | collective-permute-start | bytes 18440
  32.5 2.9 %collective-permute-start = (bf16[6,128]{1,0:T(8,128)(2,1)S(1)}, bf16[6,128]{1,0:T(8,128)(2,1)S(1)}, u32[]{:S(2)}, u32[]{:S(2)}) collective-permute-start(bf16[6,128]{1,0:T(8,128)(2,1)S(1)} %get-tuple-element.8), channel_id=1, source_target_pairs={{0,1},{2,3},{4,5},{6,7},{8,9},{10,11},{12,13},{14,15},{16,17},{18,... | collective-permute-start | bytes 4616 | tf_op jit(solution)/shard_map/ppermute | solution.py:19
  33.8 3.1 %collective-permute-start.1 = (bf16[6,128]{1,0:T(8,128)(2,1)S(1)}, bf16[6,128]{1,0:T(8,128)(2,1)S(1)}, u32[]{:S(2)}, u32[]{:S(2)}) collective-permute-start(bf16[6,128]{1,0:T(8,128)(2,1)S(1)} %get-tuple-element.9), channel_id=1, source_target_pairs={{1,0},{3,2},{5,4},{7,6},{9,8},{11,10},{13,12},{15,14},{17,16},{19,... | collective-permute-start | bytes 4616 | tf_op jit(solution)/shard_map/ppermute | solution.py:21
  37.3 55.7 %copy-start.1 = (bf16[1024,48]{0,1:T(8,128)(2,1)S(1)}, bf16[1024,48]{0,1:T(8,128)(2,1)}, u32[]{:S(2)}) copy-start(bf16[1024,48]{0,1:T(8,128)(2,1)} %param.5) | copy-start | bytes 294916
where the time goes:
time: 94.7 us; the launch traced here: 94.4 us
  blocking collectives  54.8 us (58%)
  matrix products  27.6 us (29%)
  starting transfers between devices  5.8 us (6%)
  local copies, waits for them, and re-layouts  3.02 us (3%)
  waiting for transfers between devices  1.45 us (2%)
    all_gather x1, blocking collectives, per_device(): piece = lax.all_gather(scaled, 'space', axis=0, tiled=True)  30.5 us
    conv_general_dilated x1, matrix products, band_filter(): lax.conv_general_dilated(stacked, kernel, (1,), 'VALID', feature_group_co...  24.8 us
    unnamed x1, blocking collectives  24.3 us
    unnamed x2, starting transfers between devices  3.22 us
    unnamed x12, local copies, waits for them, and re-layouts  2.06 us
  transfers between devices with their start and end apart: 4, of which 1 were waited for; matrix products, arithmetic and copies ran while one was open for 2% of the time, Pallas kernels for 0%

commit v1 on v0

v1 whole, which is shorter than its diff:
```python
import functools

import jax
import jax.numpy as jnp
from jax import lax
from jax.experimental import pallas as pl
from jax.experimental.pallas import tpu as pltpu
from jax.sharding import PartitionSpec as P

HALF = 128
WINDOW = 3 * HALF
CHUNK = 8
LAST = (((1,), (1,)), ((), ()))
FIRST = (((0,), (0,)), ((), ()))


def coefficient_kernel(columns_hbm, snapshots_hbm, out_ref, columns, snapshots, sems):
    steps = snapshots.shape[0]
    pieces = steps // HALF
    head = pltpu.make_async_copy(columns_hbm, columns, sems.at[pieces])
    copies = [
        pltpu.make_async_copy(
            snapshots_hbm.at[pl.ds(i * HALF, HALF)], snapshots.at[pl.ds(i * HALF, HALF)], sems.at[i]
        )
        for i in range(pieces)
    ]
    head.start()
    for copy in copies:
        copy.start()
    head.wait()
    for i, copy in enumerate(copies):
        copy.wait()
        span = slice(i * HALF, (i + 1) * HALF)
        out_ref[:, span] = lax.dot_general(
            columns[...], snapshots[span, :], LAST, preferred_element_type=jnp.float32
        )


def coefficients(columns, snapshots):
    rows, dofs = columns.shape
    steps = snapshots.shape[0]
    return pl.pallas_call(
        coefficient_kernel,
        out_shape=jax.ShapeDtypeStruct((rows, steps), jnp.float32),
        in_specs=[pl.BlockSpec(memory_space=pl.ANY)] * 2,
        out_specs=pl.BlockSpec(memory_space=pltpu.VMEM),
        scratch_shapes=[
            pltpu.VMEM((rows, dofs), jnp.bfloat16),
            pltpu.VMEM((steps, dofs), jnp.bfloat16),
            pltpu.SemaphoreType.DMA((steps // HALF + 1,)),
        ],
        compiler_params=pltpu.CompilerParams(vmem_limit_bytes=16 << 20),
        cost_estimate=pl.CostEstimate(
            flops=2 * rows * dofs * steps, bytes_accessed=2 * steps * dofs, transcendentals=0
        ),
        name="coefficients",
    )(columns, snapshots)


def band_kernel(taps_ref, out_ref):
    for f in range(out_ref.shape[0]):
        for part in range(2):
            row = taps_ref[2 * f + part : 2 * f + part + 1, :]
            square = jnp.broadcast_to(row, (HALF, WINDOW))
            out_ref[f, :, part * WINDOW : (part + 1) * WINDOW] = pltpu.roll(
                square, 0, 1, stride=1, stride_axis=0
            ).astype(jnp.bfloat16)


def band_matrices(filter_taps):
    freqs, parts, taps = filter_taps.shape
    padded = jnp.pad(
        filter_taps.astype(jnp.float32).reshape(freqs * parts, taps), ((0, 0), (0, WINDOW - taps))
    )
    chunk = min(CHUNK, freqs)
    return pl.pallas_call(
        band_kernel,
        grid=(freqs // chunk,),
        out_shape=jax.ShapeDtypeStruct((freqs, HALF, 2 * WINDOW), jnp.bfloat16),
        in_specs=[pl.BlockSpec((2 * chunk, WINDOW), lambda i: (i, 0))],
        out_specs=pl.BlockSpec((chunk, HALF, 2 * WINDOW), lambda i: (i, 0, 0)),
        compiler_params=pltpu.CompilerParams(vmem_limit_bytes=16 << 20),
        cost_estimate=pl.CostEstimate(
            flops=freqs * HALF * WINDOW * 40, bytes_accessed=freqs * HALF * WINDOW * 4, transcendentals=0
        ),
        name="band_matrices",
    )(padded)


def field_kernel(
    chunks, coeffs_ref, halo_ref, bands_ref, gain_ref, columns_ref, out_hbm, wide, scaled, field, total, sems
):
    rows, steps = coeffs_ref.shape
    blocks = steps // HALF
    freqs = bands_ref.shape[0]
    modes = rows // freqs
    after = lax.axis_index("tm") == 0
    halo = halo_ref[...].astype(jnp.float32)
    none = jnp.zeros_like(halo)
    cells = jnp.concatenate(
        [
            jnp.where(after, none, halo),
            coeffs_ref[...].astype(jnp.bfloat16).astype(jnp.float32),
            jnp.where(after, halo, none),
        ],
        axis=1,
    )
    cosine = lax.broadcasted_iota(jnp.int32, cells.shape, 0) % 2 == 0
    turned = jnp.where(cosine, -pltpu.roll(cells, rows - 1, 0), pltpu.roll(cells, 1, 0))
    wide[0, :rows, :] = cells
    wide[1, :rows, :] = turned
    wide[:, rows:, :] = jnp.zeros((2, 8, cells.shape[1]), jnp.float32)
    for f in range(freqs):
        at = f * modes
        own = wide[0, at : at + 8, :]
        other = wide[1, at : at + 8, :]
        inputs = jnp.concatenate(
            [
                jnp.concatenate(
                    [own[:, b * HALF : b * HALF + WINDOW], other[:, b * HALF : b * HALF + WINDOW]], axis=1
                )
                for b in range(blocks)
            ],
            axis=0,
        ).astype(jnp.bfloat16)
        filtered = lax.dot_general(inputs, bands_ref[f], LAST, preferred_element_type=jnp.float32)
        for b in range(blocks):
            scaled[at : at + 8, b * HALF : (b + 1) * HALF] = filtered[8 * b : 8 * b + 8]
    step = pl.program_id(0)
    columns = columns_ref[...]
    copies = []
    for b in range(blocks):
        span = slice(b * HALF, (b + 1) * HALF)
        piece = (scaled[:rows, span] * gain_ref[...]).astype(jnp.bfloat16)
        part = lax.dot_general(piece, columns, FIRST, preferred_element_type=jnp.float32)
        copy = pltpu.make_async_copy(field.at[pl.ds(b * HALF, HALF)], out_hbm.at[pl.ds(b * HALF, HALF)], sems.at[b])
        if chunks == 1:
            field[span, :] = part.astype(jnp.bfloat16)
            copy.start()
            copies.append(copy)
        else:

            @pl.when(step == 0)
            def _():
                total[span, :] = part

            @pl.when(step > 0)
            def _():
                total[span, :] += part

            @pl.when(step == chunks - 1)
            def _():
                field[span, :] = total[span, :].astype(jnp.bfloat16)
                copy.start()
                copy.wait()

    for copy in copies:
        copy.wait()


def band_field(coeffs, halo, bands, gain, columns):
    rows, steps = coeffs.shape
    dofs = columns.shape[1]
    freqs = bands.shape[0]
    chunk = min(CHUNK, freqs)
    chunks = freqs // chunk
    held = rows // chunks
    return pl.pallas_call(
        functools.partial(field_kernel, chunks),
        grid=(chunks,),
        out_shape=jax.ShapeDtypeStruct((steps, dofs), jnp.bfloat16),
        in_specs=[
            pl.BlockSpec((held, steps), lambda i: (i, 0)),
            pl.BlockSpec((held, HALF), lambda i: (i, 0)),
            pl.BlockSpec((chunk, HALF, 2 * WINDOW), lambda i: (i, 0, 0)),
            pl.BlockSpec((held, HALF), lambda i: (i, 0)),
            pl.BlockSpec((held, dofs), lambda i: (i, 0)),
        ],
        out_specs=pl.BlockSpec(memory_space=pl.ANY),
        scratch_shapes=[
            pltpu.VMEM((2, held + 8, steps + 2 * HALF), jnp.float32),
            pltpu.VMEM((held + 8, steps), jnp.float32),
            pltpu.VMEM((steps, dofs), jnp.bfloat16),
            pltpu.VMEM((steps if chunks > 1 else 8, dofs), jnp.float32),
            pltpu.SemaphoreType.DMA((steps // HALF,)),
        ],
        compiler_params=pltpu.CompilerParams(vmem_limit_bytes=32 << 20),
        cost_estimate=pl.CostEstimate(
            flops=2 * rows * dofs * steps, bytes_accessed=2 * steps * dofs, transcendentals=0
        ),
        name="band_field",
    )(coeffs, halo, bands, gain, columns)


def summed(values, axis):
    count = lax.axis_size(axis)
    apart = 1
    while apart < count:
        values = values + lax.ppermute(values, axis, [(i, i ^ apart) for i in range(count)])
        apart *= 2
    return values


def per_device(snapshots, mode_columns, filter_taps, mode_gain):
    columns = mode_columns.T
    gain = jnp.broadcast_to(mode_gain[:, None], (mode_gain.shape[0], HALF))
    bands = band_matrices(filter_taps)
    coeffs = summed(coefficients(columns, snapshots), "space")
    edge = jnp.where(lax.axis_index("tm") == 0, coeffs[:, -HALF:], coeffs[:, :HALF])
    halo = lax.ppermute(edge.astype(jnp.bfloat16), "tm", [(0, 1), (1, 0)])
    return band_field(coeffs, halo, bands, gain, columns)


def solution(mesh):
    placed = (P(("group", "tm"), "space"), P("space", "group"), P(), P("group"))
    return jax.shard_map(
        per_device,
        mesh=mesh,
        in_specs=placed,
        out_specs=P(("group", "tm"), "space"),
        check_vma=False,
    )
```

time: 94.7 us -> 23.1 us (0.24)
  the two profiles are of different devices: /device:TPU:0 before, /device:TPU:25 now
where the time goes in v1:
time: 23.1 us; the launch traced here: 22.9 us
  waiting for transfers between devices  11.1 us (48%)
  starting transfers between devices  5.82 us (25%)
  Pallas kernels  3.63 us (16%)
  local copies, waits for them, and re-layouts  2.23 us (10%)
    ppermute x3, waiting for transfers between devices, summed(): lax.ppermute(values, axis, [(i, i ^ apart) for i in range(count)])  10.8 us
    ppermute x1, starting transfers between devices, per_device(): halo = lax.ppermute(edge.astype(jnp.bfloat16), 'tm', [(0, 1), (1, 0)])  4.19 us
    unnamed x10, local copies, waits for them, and re-layouts  2.13 us
    pallas_call x1, Pallas kernels, band_field(): pl.pallas_call(functools.partial(field_kernel, chunks), grid=(chunks,), o...  1.89 us
    ppermute x3, starting transfers between devices, summed(): lax.ppermute(values, axis, [(i, i ^ apart) for i in range(count)])  1.63 us
    pallas_call x1, Pallas kernels, coefficients(): pl.pallas_call(coefficient_kernel, out_shape=jax.ShapeDtypeStruct((rows,...  1.27 us
    pallas_call x1, Pallas kernels, band_matrices(): pl.pallas_call(band_kernel, grid=(freqs // chunk,), out_shape=jax.ShapeDt...  0.47 us
  transfers between devices with their start and end apart: 4, of which 4 were waited for; matrix products, arithmetic and copies ran while one was open for 0% of the time, Pallas kernels for 2%

profile of v1, /device:TPU:25, one launch (start us, length us, event | category | flops | bytes accessed | tf_op | source)
XLA Modules:
  0.0 22.9 jit_solution(3461496826859950405)
XLA Ops:
  0.0 0.0 copy-start
  0.0 1.2 %copy-done = bf16[512,1024]{1,0:T(8,128)(2,1)S(1)} copy-done((bf16[512,1024]{1,0:T(8,128)(2,1)S(1)}, bf16[512,1024]{1,0:T(8,128)(2,1)}, u32[]{:S(2)}) %copy-start) | copy-done | bytes 1048600
  1.2 0.0 copy-start.1
  1.2 0.9 %copy-done.1 = bf16[1024,48]{0,1:T(8,128)(2,1)S(1)} copy-done((bf16[1024,48]{0,1:T(8,128)(2,1)S(1)}, bf16[1024,48]{0,1:T(8,128)(2,1)}, u32[]{:S(2)}) %copy-start.1) | copy-done | bytes 98328
  2.1 0.0 copy-start.3
  2.1 1.3 %coefficients.1 = f32[48,512]{1,0:T(8,128)S(1)} custom-call(bf16[48,1024]{1,0:T(8,128)(2,1)S(1)} %bitcast.1, bf16[512,1024]{1,0:T(8,128)(2,1)S(1)} %copy-done), custom_call_target="tpu_custom_call" | custom-call | flops 50331648 | bytes 1048576 | tf_op jit(solution)/shard_map/coefficients/pallas_call | solution.py:42
  3.4 0.0 copy-start.4
  3.4 0.0 copy-start.2
  3.4 1.3 %collective-permute-start = (f32[48,512]{1,0:T(8,128)S(1)}, f32[48,512]{1,0:T(8,128)S(1)}, u32[]{:S(2)}, u32[]{:S(2)}) collective-permute-start(f32[48,512]{1,0:T(8,128)S(1)} %coefficients.1), channel_id=1, source_target_pairs={{0,2},{2,0},{4,6},{6,4},{8,10},{10,8},{12,14},{14,12},{1,3},{3,1},... | collective-permute-start | bytes 294920 | tf_op jit(solution)/shard_map/ppermute | solution.py:199
  4.7 2.3 %collective-permute-done = f32[48,512]{1,0:T(8,128)S(1)} collective-permute-done((f32[48,512]{1,0:T(8,128)S(1)}, f32[48,512]{1,0:T(8,128)S(1)}, u32[]{:S(2)}, u32[]{:S(2)}) %collective-permute-start) | collective-permute-done | bytes 98336 | tf_op jit(solution)/shard_map/ppermute | solution.py:199
  7.0 0.2 %collective-permute-start.1 = (f32[48,512]{1,0:T(8,128)S(1)}, f32[48,512]{1,0:T(8,128)S(1)}, u32[]{:S(2)}, u32[]{:S(2)}) collective-permute-start(f32[48,512]{1,0:T(8,128)S(1)} %add.11), channel_id=1, source_target_pairs={{0,4},{2,6},{4,0},{6,2},{8,12},{10,14},{12,8},{14,10},{1,5},{3,7},... | collective-permute-start | bytes 294920 | tf_op jit(solution)/shard_map/ppermute | solution.py:199
  7.2 3.3 %collective-permute-done.1 = f32[48,512]{1,0:T(8,128)S(1)} collective-permute-done((f32[48,512]{1,0:T(8,128)S(1)}, f32[48,512]{1,0:T(8,128)S(1)}, u32[]{:S(2)}, u32[]{:S(2)}) %collective-permute-start.1) | collective-permute-done | bytes 98336 | tf_op jit(solution)/shard_map/ppermute | solution.py:199
  10.5 0.1 collective-permute-start.2
  10.6 0.0 copy-done.3
  10.7 5.2 %collective-permute-done.2 = f32[48,512]{1,0:T(8,128)S(1)} collective-permute-done((f32[48,512]{1,0:T(8,128)S(1)}, f32[48,512]{1,0:T(8,128)S(1)}, u32[]{:S(2)}, u32[]{:S(2)}) %collective-permute-start.2) | collective-permute-done | bytes 98336 | tf_op jit(solution)/shard_map/ppermute | solution.py:199
  15.9 4.2 %collective-permute-start.3 = (bf16[48,128]{1,0:T(8,128)(2,1)S(1)}, bf16[48,128]{1,0:T(8,128)(2,1)S(1)}, u32[]{:S(2)}, u32[]{:S(2)}) collective-permute-start(bf16[48,128]{1,0:T(8,128)(2,1)S(1)} %fusion), channel_id=1, source_target_pairs={{0,1},{1,0},{2,3},{3,2},{4,5},{5,4},{6,7},{7,6},{8,9},{9,8},{10,11... | collective-permute-start | bytes 36872 | tf_op jit(solution)/shard_map/ppermute | solution.py:210
  20.1 0.5 %band_matrices.1.bands_ref = bf16[8,128,768]{2,1,0:T(8,128)(2,1)S(1)} custom-call(f32[16,384]{1,0:T(8,128)S(1)} %pad_convert_fusion.taps_ref), custom_call_target="tpu_custom_call" | custom-call | flops 15728640 | bytes 1572864 | tf_op jit(solution)/shard_map/band_matrices/pallas_call | solution.py:76
  20.6 0.3 %collective-permute-done.3.halo_ref = bf16[48,128]{1,0:T(8,128)(2,1)S(1)} collective-permute-done((bf16[48,128]{1,0:T(8,128)(2,1)S(1)}, bf16[48,128]{1,0:T(8,128)(2,1)S(1)}, u32[]{:S(2)}, u32[]{:S(2)}) %collective-permute-start.3) | collective-permute-done | bytes 12320 | tf_op jit(solution)/shard_map/ppermute | solution.py:210
  20.9 0.0 copy-done.4
  21.0 0.1 broadcast_in_dim.2.gain_ref
  21.0 0.0 copy-done.2
  21.0 1.9 %band_field.1 = bf16[512,1024]{1,0:T(8,128)(2,1)} custom-call(f32[48,512]{1,0:T(8,128)S(1)} %add.13.coeffs_ref, bf16[48,128]{1,0:T(8,128)(2,1)S(1)} %collective-permute-done.3.halo_ref, bf16[8,128,768]{2,1,0:T(8,128)(2,1)S(1)} %band_matrices.1.bands_ref, f32[48,128]{1,0:T(8,128)S(1)} %broadcast_in_dim.2.gain_ref, bf16[48,1024]{1,0:T(8,128)(2,1)S(1)} %bitcast.2), custom_call_target="tpu_custom_call" | custom-call | flops 50331648 | bytes 1048576 | tf_op jit(solution)/shard_map/band_field/pallas_call | solution.py:168
  (6 shorter events, 0.1 us)
Async XLA Ops:
  0.0 1.2 %copy-start = (bf16[512,1024]{1,0:T(8,128)(2,1)S(1)}, bf16[512,1024]{1,0:T(8,128)(2,1)}, u32[]{:S(2)}) copy-start(bf16[512,1024]{1,0:T(8,128)(2,1)} %snapshots_hbm.1) | copy-start | bytes 3145732
  1.2 0.9 %copy-start.1 = (bf16[1024,48]{0,1:T(8,128)(2,1)S(1)}, bf16[1024,48]{0,1:T(8,128)(2,1)}, u32[]{:S(2)}) copy-start(bf16[1024,48]{0,1:T(8,128)(2,1)} %param.5) | copy-start | bytes 294916
  2.1 8.5 %copy-start.3 = (bf16[8,2,257]{2,1,0:T(2,128)(2,1)S(1)}, bf16[8,2,257]{2,1,0:T(2,128)(2,1)}, u32[]{:S(2)}) copy-start(bf16[8,2,257]{2,1,0:T(2,128)(2,1)} %param.6) | copy-start | bytes 24676
  3.4 17.6 %copy-start.4 = (f32[48]{0:T(128)S(1)}, f32[48]{0:T(128)}, u32[]{:S(2)}) copy-start(f32[48]{0:T(128)} %param.7) | copy-start | bytes 580
  3.4 17.6 %copy-start.2 = (bf16[1024,48]{0,1:T(8,128)(2,1)S(1)}, bf16[1024,48]{0,1:T(8,128)(2,1)}, u32[]{:S(2)}) copy-start(bf16[1024,48]{0,1:T(8,128)(2,1)} %param.5) | copy-start | bytes 294916
  3.4 3.5 %collective-permute-start = (f32[48,512]{1,0:T(8,128)S(1)}, f32[48,512]{1,0:T(8,128)S(1)}, u32[]{:S(2)}, u32[]{:S(2)}) collective-permute-start(f32[48,512]{1,0:T(8,128)S(1)} %coefficients.1), channel_id=1, source_target_pairs={{0,2},{2,0},{4,6},{6,4},{8,10},{10,8},{12,14},{14,12},{1,3},{3,1},... | collective-permute-start | bytes 294920 | tf_op jit(solution)/shard_map/ppermute | solution.py:199
  7.0 3.5 %collective-permute-start.1 = (f32[48,512]{1,0:T(8,128)S(1)}, f32[48,512]{1,0:T(8,128)S(1)}, u32[]{:S(2)}, u32[]{:S(2)}) collective-permute-start(f32[48,512]{1,0:T(8,128)S(1)} %add.11), channel_id=1, source_target_pairs={{0,4},{2,6},{4,0},{6,2},{8,12},{10,14},{12,8},{14,10},{1,5},{3,7},... | collective-permute-start | bytes 294920 | tf_op jit(solution)/shard_map/ppermute | solution.py:199
  10.5 5.4 %collective-permute-start.2 = (f32[48,512]{1,0:T(8,128)S(1)}, f32[48,512]{1,0:T(8,128)S(1)}, u32[]{:S(2)}, u32[]{:S(2)}) collective-permute-start(f32[48,512]{1,0:T(8,128)S(1)} %add.12), channel_id=1, source_target_pairs={{0,8},{2,10},{4,12},{6,14},{8,0},{10,2},{12,4},{14,6},{1,9},{3,11}... | collective-permute-start | bytes 294920 | tf_op jit(solution)/shard_map/ppermute | solution.py:199
  15.9 5.0 %collective-permute-start.3 = (bf16[48,128]{1,0:T(8,128)(2,1)S(1)}, bf16[48,128]{1,0:T(8,128)(2,1)S(1)}, u32[]{:S(2)}, u32[]{:S(2)}) collective-permute-start(bf16[48,128]{1,0:T(8,128)(2,1)S(1)} %fusion), channel_id=1, source_target_pairs={{0,1},{1,0},{2,3},{3,2},{4,5},{5,4},{6,7},{7,6},{8,9},{9,8},{10,11... | collective-permute-start | bytes 36872 | tf_op jit(solution)/shard_map/ppermute | solution.py:210

commit v2 on v1

v2 whole, which is shorter than its diff:
```python
import functools
import math

import jax
import jax.numpy as jnp
from jax import lax
from jax.experimental import pallas as pl
from jax.experimental.pallas import tpu as pltpu
from jax.sharding import PartitionSpec as P

HALF = 128
WINDOW = 3 * HALF
CHUNK = 8
SPLITS = 4
LAST = (((1,), (1,)), ((), ()))
FIRST = (((0,), (0,)), ((), ()))
WHOLE = pl.BlockSpec(memory_space=pltpu.VMEM)


def coefficient_kernel(columns_hbm, snapshots_hbm, out_ref, columns, snapshots, sems):
    width = snapshots.shape[1] // SPLITS
    head = pltpu.make_async_copy(columns_hbm, columns, sems.at[SPLITS])
    head.start()
    copies = []
    for i in range(SPLITS):
        span = pl.ds(i * width, width)
        copies.append(pltpu.make_async_copy(snapshots_hbm.at[:, span], snapshots.at[:, span], sems.at[i]))
        copies[-1].start()
    head.wait()
    total = None
    for i, copy in enumerate(copies):
        copy.wait()
        span = slice(i * width, (i + 1) * width)
        part = lax.dot_general(columns[:, span], snapshots[:, span], LAST, preferred_element_type=jnp.float32)
        total = part if total is None else total + part
    out_ref[...] = total


def coefficients(columns, snapshots):
    rows, dofs = columns.shape
    steps = snapshots.shape[0]
    return pl.pallas_call(
        coefficient_kernel,
        out_shape=pltpu.VMEM((rows, steps), jnp.float32),
        in_specs=[pl.BlockSpec(memory_space=pltpu.HBM)] * 2,
        out_specs=WHOLE,
        scratch_shapes=[
            pltpu.VMEM((rows, dofs), jnp.bfloat16),
            pltpu.VMEM((steps, dofs), jnp.bfloat16),
            pltpu.SemaphoreType.DMA((SPLITS + 1,)),
        ],
        compiler_params=pltpu.CompilerParams(vmem_limit_bytes=16 << 20),
        cost_estimate=pl.CostEstimate(
            flops=2 * rows * dofs * steps, bytes_accessed=2 * steps * dofs, transcendentals=0
        ),
        name="coefficients",
    )(pltpu.with_memory_space_constraint(columns, pltpu.HBM), pltpu.with_memory_space_constraint(snapshots, pltpu.HBM))


def band_kernel(taps_ref, out_ref):
    for f in range(out_ref.shape[0]):
        for part in range(2):
            row = taps_ref[2 * f + part : 2 * f + part + 1, :]
            square = jnp.broadcast_to(row, (HALF, WINDOW))
            out_ref[f, :, part * WINDOW : (part + 1) * WINDOW] = pltpu.roll(
                square, 0, 1, stride=1, stride_axis=0
            ).astype(jnp.bfloat16)


def padded_taps(filter_taps):
    freqs, parts, taps = filter_taps.shape
    rows = filter_taps.astype(jnp.float32).reshape(freqs * parts, taps)
    return jnp.pad(rows, ((0, 0), (0, WINDOW - taps)))


def band_matrices(taps):
    freqs = taps.shape[0] // 2
    chunk = min(CHUNK, freqs)
    one = freqs == chunk
    shape = (freqs, HALF, 2 * WINDOW)
    return pl.pallas_call(
        band_kernel,
        grid=() if one else (freqs // chunk,),
        out_shape=pltpu.VMEM(shape, jnp.bfloat16) if one else jax.ShapeDtypeStruct(shape, jnp.bfloat16),
        in_specs=[WHOLE if one else pl.BlockSpec((2 * chunk, WINDOW), lambda i: (i, 0))],
        out_specs=WHOLE if one else pl.BlockSpec((chunk, HALF, 2 * WINDOW), lambda i: (i, 0, 0)),
        compiler_params=pltpu.CompilerParams(vmem_limit_bytes=16 << 20),
        cost_estimate=pl.CostEstimate(
            flops=freqs * HALF * WINDOW * 40, bytes_accessed=freqs * HALF * WINDOW * 4, transcendentals=0
        ),
        name="band_matrices",
    )(taps)


def turned(cells):
    cosine = lax.broadcasted_iota(jnp.int32, cells.shape, 0) % 2 == 0
    return jnp.where(cosine, -pltpu.roll(cells, cells.shape[0] - 1, 0), pltpu.roll(cells, 1, 0))


def add_over_chunks(chunks, total, span, part, store):
    if chunks == 1:
        store(part)
        return
    step = pl.program_id(0)
    total[span, :] = jnp.where(step == 0, part, total[span, :] + part)

    @pl.when(step == chunks - 1)
    def _():
        store(total[span, :])


def own_kernel(chunks, coeffs_ref, bands_ref, gain_ref, columns_ref, filtered_ref, field_ref, wide, total):
    rows, steps = coeffs_ref.shape
    blocks = steps // HALF
    freqs = bands_ref.shape[0]
    modes = rows // freqs
    cells = coeffs_ref[...].astype(jnp.bfloat16).astype(jnp.float32)
    for i, part in enumerate((cells, turned(cells))):
        wide[i, :, :HALF] = jnp.zeros((rows + 8, HALF), jnp.float32)
        wide[i, :, HALF + steps :] = jnp.zeros((rows + 8, HALF), jnp.float32)
        wide[i, :rows, HALF : HALF + steps] = part
        wide[i, rows:, HALF : HALF + steps] = jnp.zeros((8, steps), jnp.float32)
    for f in range(freqs):
        at = f * modes
        both = [wide[i, at : at + 8, :] for i in range(2)]
        inputs = jnp.concatenate(
            [
                jnp.concatenate([part[:, b * HALF : b * HALF + WINDOW] for part in both], axis=1)
                for b in range(blocks)
            ],
            axis=0,
        ).astype(jnp.bfloat16)
        filtered = lax.dot_general(inputs, bands_ref[f], LAST, preferred_element_type=jnp.float32)
        for b in range(blocks):
            filtered_ref[at : at + modes, b * HALF : (b + 1) * HALF] = filtered[8 * b : 8 * b + modes]
    columns = columns_ref[...]
    for b in range(blocks):
        span = slice(b * HALF, (b + 1) * HALF)
        piece = (filtered_ref[:, span] * gain_ref[...]).astype(jnp.bfloat16)
        part = lax.dot_general(piece, columns, FIRST, preferred_element_type=jnp.float32)

        def store(values, span=span):
            field_ref[span, :] = values.astype(jnp.bfloat16)

        add_over_chunks(chunks, total, span, part, store)


def edge_kernel(
    chunks, halo_ref, filtered_ref, bands_ref, gain_ref, columns_ref, field_ref, out_hbm, wide, more, edge, total, sems
):
    rows, steps = filtered_ref.shape
    freqs = bands_ref.shape[0]
    modes = rows // freqs
    after = lax.axis_index("tm") == 0
    place = pl.multiple_of(jnp.where(after, steps - HALF, 0), HALF)
    rest = pl.multiple_of(jnp.where(after, 0, HALF), HALF)
    reach = pl.multiple_of(jnp.where(after, WINDOW - HALF, 0), HALF)
    first = pltpu.make_async_copy(
        field_ref.at[pl.ds(rest, steps - HALF)], out_hbm.at[pl.ds(rest, steps - HALF)], sems.at[0]
    )
    last = pltpu.make_async_copy(edge, out_hbm.at[pl.ds(place, HALF)], sems.at[1])
    if chunks == 1:
        first.start()
    cells = halo_ref[...].astype(jnp.float32)
    for i, part in enumerate((cells, turned(cells))):
        wide[i, :rows, :] = part
        wide[i, rows:, :] = jnp.zeros((8, HALF), jnp.float32)
    for f in range(freqs):
        at = f * modes
        inputs = jnp.concatenate([wide[i, at : at + 8, :] for i in range(2)], axis=1).astype(jnp.bfloat16)
        taps = jnp.concatenate(
            [bands_ref[f, :, pl.ds(pl.multiple_of(reach + i * WINDOW, HALF), HALF)] for i in range(2)], axis=1
        )
        filtered = lax.dot_general(inputs, taps, LAST, preferred_element_type=jnp.float32)
        more[at : at + modes, :] = filtered[:modes]
    piece = ((filtered_ref[:, pl.ds(place, HALF)] + more[...]) * gain_ref[...]).astype(jnp.bfloat16)
    part = lax.dot_general(piece, columns_ref[...], FIRST, preferred_element_type=jnp.float32)

    def store(values):
        edge[...] = values.astype(jnp.bfloat16)
        last.start()
        if chunks > 1:
            first.start()
        first.wait()
        last.wait()

    add_over_chunks(chunks, total, slice(0, HALF), part, store)


def band_field(coeffs, halo, bands, gain, columns):
    rows, steps = coeffs.shape
    dofs = columns.shape[1]
    freqs = bands.shape[0]
    chunk = min(CHUNK, freqs)
    chunks = freqs // chunk
    one = chunks == 1
    held = rows // chunks
    grid = () if one else (chunks,)
    made = pltpu.VMEM if one else jax.ShapeDtypeStruct

    def rows_of(width):
        return WHOLE if one else pl.BlockSpec((held, width), lambda i: (i, 0))

    taps = WHOLE if one else pl.BlockSpec((chunk, HALF, 2 * WINDOW), lambda i: (i, 0, 0))
    params = pltpu.CompilerParams(vmem_limit_bytes=24 << 20)
    filtered, field = pl.pallas_call(
        functools.partial(own_kernel, chunks),
        grid=grid,
        out_shape=[made((rows, steps), jnp.float32), made((steps, dofs), jnp.bfloat16)],
        in_specs=[rows_of(steps), taps, rows_of(HALF), rows_of(dofs)],
        out_specs=[rows_of(steps), WHOLE],
        scratch_shapes=[
            pltpu.VMEM((2, held + 8, steps + 2 * HALF), jnp.float32),
            pltpu.VMEM((8 if one else steps, dofs), jnp.float32),
        ],
        compiler_params=params,
        cost_estimate=pl.CostEstimate(
            flops=2 * rows * dofs * steps, bytes_accessed=2 * steps * dofs, transcendentals=0
        ),
        name="own_field",
    )(coeffs, bands, gain, columns)
    return pl.pallas_call(
        functools.partial(edge_kernel, chunks),
        grid=grid,
        out_shape=jax.ShapeDtypeStruct((steps, dofs), jnp.bfloat16),
        in_specs=[rows_of(HALF), rows_of(steps), taps, rows_of(HALF), rows_of(dofs), WHOLE],
        out_specs=pl.BlockSpec(memory_space=pl.ANY),
        scratch_shapes=[
            pltpu.VMEM((2, held + 8, HALF), jnp.float32),
            pltpu.VMEM((held, HALF), jnp.float32),
            pltpu.VMEM((HALF, dofs), jnp.bfloat16),
            pltpu.VMEM((8 if one else HALF, dofs), jnp.float32),
            pltpu.SemaphoreType.DMA((2,)),
        ],
        compiler_params=params,
        cost_estimate=pl.CostEstimate(
            flops=2 * rows * dofs * HALF, bytes_accessed=2 * steps * dofs, transcendentals=0
        ),
        name="edge_field",
    )(halo, filtered, bands, gain, columns, field)


def message_scale(dofs, all_dofs):
    snapshot, column = 6.0, 0.0625 * math.sqrt(8192 / all_dofs)
    return 2.0 ** math.floor(math.log2(65504 / (dofs * snapshot * column)))


def exchanged(values, axis, apart, scale):
    count = lax.axis_size(axis)
    message = (values * scale).astype(jnp.float16)
    other = lax.ppermute(message, axis, [(i, i ^ apart) for i in range(count)])
    return values + other.astype(jnp.float32) * (1 / scale)


def per_device(snapshots, mode_columns, filter_taps, mode_gain):
    columns = mode_columns.T
    devices = lax.axis_size("space")
    dofs = columns.shape[1]
    taps = padded_taps(filter_taps)
    gain = jnp.broadcast_to(mode_gain[:, None], (mode_gain.shape[0], HALF))
    coeffs = coefficients(columns, snapshots)
    apart = 1
    while 2 * apart < devices:
        if apart == 2:
            coeffs, taps = lax.optimization_barrier((coeffs, taps))
        coeffs = exchanged(coeffs, "space", apart, message_scale(dofs * apart, dofs * devices))
        apart *= 2
    bands = band_matrices(taps)
    coeffs, bands, gain = lax.optimization_barrier((coeffs, bands, gain))
    coeffs = exchanged(coeffs, "space", apart, message_scale(dofs * apart, dofs * devices))
    edge = jnp.where(lax.axis_index("tm") == 0, coeffs[:, -HALF:], coeffs[:, :HALF])
    halo = lax.ppermute(edge.astype(jnp.bfloat16), "tm", [(0, 1), (1, 0)])
    return band_field(coeffs, halo, bands, gain, columns)


def solution(mesh):
    placed = (P(("group", "tm"), "space"), P("space", "group"), P(), P("group"))
    return jax.shard_map(
        per_device,
        mesh=mesh,
        in_specs=placed,
        out_specs=P(("group", "tm"), "space"),
        check_vma=False,
    )
```

time: 23.1 us -> 19 us (0.82)
  waiting for transfers between devices: 11.1 us -> 7.48 us
  local copies, waits for them, and re-layouts: 2.23 us -> 0.81 us
  Pallas kernels: 3.63 us -> 4.39 us
    ppermute x3, waiting for transfers between devices: 10.8 us -> 7.47 us  [exchanged(): other = lax.ppermute(message, axis, [(i, i ^ apart) for i in range(count)])]
    unnamed x10 -> x4, local copies, waits for them, and re-layouts: 2.13 us -> 0.01 us
    pallas_call x3 -> x4, Pallas kernels: 3.63 us -> 4.39 us  [the longest x1 1.6 us: coefficients(): pl.pallas_call(coefficient_kernel, out_shape=pltpu.VMEM((rows, steps), jn...]
    reshape x1, local copies, waits for them, and re-layouts: 0.02 us -> 0.73 us  [padded_taps(): rows = filter_taps.astype(jnp.float32).reshape(freqs * parts, taps)]
    ppermute x1, waiting for transfers between devices: 0.34 us -> 0.01 us  [per_device(): halo = lax.ppermute(edge.astype(jnp.bfloat16), 'tm', [(0, 1), (1, 0)])]
  transfers between devices with their start and end apart: 4 -> 4, of which waited for: 4 -> 3; matrix products, arithmetic and copies ran while one was open for 0% -> 4% of each run, Pallas kernels for 2% -> 8%
where the time goes in v2:
time: 19 us; the launch traced here: 18.7 us
  waiting for transfers between devices  7.48 us (39%)
  starting transfers between devices  5.82 us (31%)
  Pallas kernels  4.39 us (23%)
  local copies, waits for them, and re-layouts  0.81 us (4%)
    ppermute x3, waiting for transfers between devices, exchanged(): other = lax.ppermute(message, axis, [(i, i ^ apart) for i in range(count)])  7.47 us
    ppermute x1, starting transfers between devices, per_device(): halo = lax.ppermute(edge.astype(jnp.bfloat16), 'tm', [(0, 1), (1, 0)])  4.19 us
    ppermute x3, starting transfers between devices, exchanged(): other = lax.ppermute(message, axis, [(i, i ^ apart) for i in range(count)])  1.63 us
    pallas_call x1, Pallas kernels, coefficients(): pl.pallas_call(coefficient_kernel, out_shape=pltpu.VMEM((rows, steps), jn...  1.6 us
    pallas_call x1, Pallas kernels, band_field(): pl.pallas_call(functools.partial(edge_kernel, chunks), grid=grid, out_sha...  1.24 us
    pallas_call x1, Pallas kernels, band_field(): pl.pallas_call(functools.partial(own_kernel, chunks), grid=grid, out_shap...  1.09 us
    reshape x1, local copies, waits for them, and re-layouts, padded_taps(): rows = filter_taps.astype(jnp.float32).reshape(freqs * parts, taps)  0.73 us
    pallas_call x1, Pallas kernels, band_matrices(): pl.pallas_call(band_kernel, grid=() if one else (freqs // chunk,), out_sh...  0.47 us
  transfers between devices with their start and end apart: 4, of which 3 were waited for; matrix products, arithmetic and copies ran while one was open for 4% of the time, Pallas kernels for 8%

profile of v2, /device:TPU:25, one launch (start us, length us, event | category | flops | bytes accessed | tf_op | source)
XLA Modules:
  0.0 18.7 jit_solution(9655866060395922487)
XLA Ops:
  0.0 0.0 copy-start.1
  0.0 1.6 %coefficients.1 = f32[48,512]{1,0:T(8,128)S(1)} custom-call(bf16[48,1024]{1,0:T(8,128)(2,1)} %bitcast.1, bf16[512,1024]{1,0:T(8,128)(2,1)} %snapshots_hbm.1), custom_call_target="tpu_custom_call" | custom-call | flops 50331648 | bytes 1048576 | tf_op jit(solution)/shard_map/coefficients/pallas_call | solution.py:42
  1.6 0.0 copy-start
  1.6 1.3 %collective-permute-start = (f16[48,512]{1,0:T(8,128)(2,1)S(1)}, f16[48,512]{1,0:T(8,128)(2,1)S(1)}, u32[]{:S(2)}, u32[]{:S(2)}) collective-permute-start(f16[48,512]{1,0:T(8,128)(2,1)S(1)} %multiply_convert_fusion.2), channel_id=1, source_target_pairs={{0,2},{2,0},{4,6},{6,4},{8,10},{10,8},{12,14},{14,12},{1,3},{3,1},... | collective-permute-start | bytes 147464 | tf_op jit(solution)/shard_map/ppermute | solution.py:251
  2.9 0.7 %reshape.5 = bf16[16,257]{1,0:T(8,128)(2,1)S(1)} reshape(bf16[8,2,257]{2,1,0:T(2,128)(2,1)} %param.6) | data formatting | bytes 16448 | tf_op jit(solution)/shard_map/reshape | solution.py:72
  3.7 1.0 %collective-permute-done = f16[48,512]{1,0:T(8,128)(2,1)S(1)} collective-permute-done((f16[48,512]{1,0:T(8,128)(2,1)S(1)}, f16[48,512]{1,0:T(8,128)(2,1)S(1)}, u32[]{:S(2)}, u32[]{:S(2)}) %collective-permute-start) | collective-permute-done | bytes 49184 | tf_op jit(solution)/shard_map/ppermute | solution.py:251
  4.7 0.2 %collective-permute-start.1 = (f16[48,512]{1,0:T(8,128)(2,1)S(1)}, f16[48,512]{1,0:T(8,128)(2,1)S(1)}, u32[]{:S(2)}, u32[]{:S(2)}) collective-permute-start(f16[48,512]{1,0:T(8,128)(2,1)S(1)} %multiply_convert_fusion.1), channel_id=1, source_target_pairs={{0,4},{2,6},{4,0},{6,2},{8,12},{10,14},{12,8},{14,10},{1,5},{3,7},... | collective-permute-start | bytes 147464 | tf_op jit(solution)/shard_map/ppermute | solution.py:251
  4.9 0.5 %band_matrices.1.bands_ref = bf16[8,128,768]{2,1,0:T(8,128)(2,1)S(1)} custom-call(f32[16,384]{1,0:T(8,128)S(1)} %pad_convert_fusion.taps_ref), custom_call_target="tpu_custom_call" | custom-call | flops 15728640 | bytes 1572864 | tf_op jit(solution)/shard_map/band_matrices/pallas_call | solution.py:81
  5.4 2.3 %collective-permute-done.1 = f16[48,512]{1,0:T(8,128)(2,1)S(1)} collective-permute-done((f16[48,512]{1,0:T(8,128)(2,1)S(1)}, f16[48,512]{1,0:T(8,128)(2,1)S(1)}, u32[]{:S(2)}, u32[]{:S(2)}) %collective-permute-start.1) | collective-permute-done | bytes 49184 | tf_op jit(solution)/shard_map/ppermute | solution.py:251
  7.7 0.0 copy-done.1
  7.7 0.1 broadcast_in_dim.2.gain_ref
  7.8 0.1 collective-permute-start.2
  7.9 4.2 %collective-permute-done.2 = f16[48,512]{1,0:T(8,128)(2,1)S(1)} collective-permute-done((f16[48,512]{1,0:T(8,128)(2,1)S(1)}, f16[48,512]{1,0:T(8,128)(2,1)S(1)}, u32[]{:S(2)}, u32[]{:S(2)}) %collective-permute-start.2) | collective-permute-done | bytes 49184 | tf_op jit(solution)/shard_map/ppermute | solution.py:251
  12.2 4.2 %collective-permute-start.3 = (bf16[48,128]{1,0:T(8,128)(2,1)S(1)}, bf16[48,128]{1,0:T(8,128)(2,1)S(1)}, u32[]{:S(2)}, u32[]{:S(2)}) collective-permute-start(bf16[48,128]{1,0:T(8,128)(2,1)S(1)} %fusion), channel_id=1, source_target_pairs={{0,1},{1,0},{2,3},{3,2},{4,5},{5,4},{6,7},{7,6},{8,9},{9,8},{10,11... | collective-permute-start | bytes 36872 | tf_op jit(solution)/shard_map/ppermute | solution.py:272
  16.3 0.0 copy-done
  16.4 1.1 %own_field.1 = (f32[48,512]{1,0:T(8,128)S(1)}, bf16[512,1024]{1,0:T(8,128)(2,1)S(1)}) custom-call(f32[48,512]{1,0:T(8,128)S(1)} %multiply_add_fusion.coeffs_ref, bf16[8,128,768]{2,1,0:T(8,128)(2,1)S(1)} %band_matrices.1.bands_ref, f32[48,128]{1,0:T(8,128)S(1)} %broadcast_in_dim.2.gain_ref, bf16[48,1024]{1,0:T(8,128)(2,1)S(1)} %bitcast.2), custom_call_target="tpu_custom_call" | custom-call | flops 50331648 | bytes 1048576 | tf_op jit(solution)/shard_map/own_field/pallas_call | solution.py:206
  17.4 0.0 collective-permute-done.3.halo_ref
  17.5 1.2 %edge_field.1 = bf16[512,1024]{1,0:T(8,128)(2,1)} custom-call(bf16[48,128]{1,0:T(8,128)(2,1)S(1)} %collective-permute-done.3.halo_ref, f32[48,512]{1,0:T(8,128)S(1)} %get-tuple-element.17.filtered_ref, bf16[8,128,768]{2,1,0:T(8,128)(2,1)S(1)} %band_matrices.1.bands_ref, f32[48,128]{1,0:T(8,128)S(1)} %broadcast_in_dim.2.gain_ref, ...), custom_call_target="tpu_custom_call" | custom-call | flops 12582912 | bytes 1048576 | tf_op jit(solution)/shard_map/edge_field/pallas_call | solution.py:222
  (8 shorter events, 0.1 us)
Async XLA Ops:
  0.0 7.7 %copy-start.1 = (f32[48]{0:T(128)S(1)}, f32[48]{0:T(128)}, u32[]{:S(2)}) copy-start(f32[48]{0:T(128)} %param.7) | copy-start | bytes 580
  1.6 14.7 %copy-start = (bf16[1024,48]{0,1:T(8,128)(2,1)S(1)}, bf16[1024,48]{0,1:T(8,128)(2,1)}, u32[]{:S(2)}) copy-start(bf16[1024,48]{0,1:T(8,128)(2,1)} %param.5) | copy-start | bytes 294916
  1.6 3.0 %collective-permute-start = (f16[48,512]{1,0:T(8,128)(2,1)S(1)}, f16[48,512]{1,0:T(8,128)(2,1)S(1)}, u32[]{:S(2)}, u32[]{:S(2)}) collective-permute-start(f16[48,512]{1,0:T(8,128)(2,1)S(1)} %multiply_convert_fusion.2), channel_id=1, source_target_pairs={{0,2},{2,0},{4,6},{6,4},{8,10},{10,8},{12,14},{14,12},{1,3},{3,1},... | collective-permute-start | bytes 147464 | tf_op jit(solution)/shard_map/ppermute | solution.py:251
  4.7 3.0 %collective-permute-start.1 = (f16[48,512]{1,0:T(8,128)(2,1)S(1)}, f16[48,512]{1,0:T(8,128)(2,1)S(1)}, u32[]{:S(2)}, u32[]{:S(2)}) collective-permute-start(f16[48,512]{1,0:T(8,128)(2,1)S(1)} %multiply_convert_fusion.1), channel_id=1, source_target_pairs={{0,4},{2,6},{4,0},{6,2},{8,12},{10,14},{12,8},{14,10},{1,5},{3,7},... | collective-permute-start | bytes 147464 | tf_op jit(solution)/shard_map/ppermute | solution.py:251
  7.8 4.3 %collective-permute-start.2 = (f16[48,512]{1,0:T(8,128)(2,1)S(1)}, f16[48,512]{1,0:T(8,128)(2,1)S(1)}, u32[]{:S(2)}, u32[]{:S(2)}) collective-permute-start(f16[48,512]{1,0:T(8,128)(2,1)S(1)} %multiply_convert_fusion), channel_id=1, source_target_pairs={{0,8},{2,10},{4,12},{6,14},{8,0},{10,2},{12,4},{14,6},{1,9},{3,11}... | collective-permute-start | bytes 147464 | tf_op jit(solution)/shard_map/ppermute | solution.py:251
  12.2 5.3 %collective-permute-start.3 = (bf16[48,128]{1,0:T(8,128)(2,1)S(1)}, bf16[48,128]{1,0:T(8,128)(2,1)S(1)}, u32[]{:S(2)}, u32[]{:S(2)}) collective-permute-start(bf16[48,128]{1,0:T(8,128)(2,1)S(1)} %fusion), channel_id=1, source_target_pairs={{0,1},{1,0},{2,3},{3,2},{4,5},{5,4},{6,7},{7,6},{8,9},{9,8},{10,11... | collective-permute-start | bytes 36872 | tf_op jit(solution)/shard_map/ppermute | solution.py:272

commit v3 on v2

--- a/solution.py
+++ b/solution.py
@@ -109,10 +109,12 @@
         store(total[span, :])
 
 
-def own_kernel(chunks, coeffs_ref, bands_ref, gain_ref, columns_ref, filtered_ref, field_ref, wide, total):
+def own_kernel(chunks, parts, coeffs_ref, *refs):
+    bands, (gain_ref, columns_ref, filtered_ref, field_ref, wide, total) = refs[:parts], refs[parts:]
     rows, steps = coeffs_ref.shape
     blocks = steps // HALF
-    freqs = bands_ref.shape[0]
+    each = bands[0].shape[0]
+    freqs = parts * each
     modes = rows // freqs
     cells = coeffs_ref[...].astype(jnp.bfloat16).astype(jnp.float32)
     for i, part in enumerate((cells, turned(cells))):
@@ -130,7 +132,8 @@
             ],
             axis=0,
         ).astype(jnp.bfloat16)
-        filtered = lax.dot_general(inputs, bands_ref[f], LAST, preferred_element_type=jnp.float32)
+        band = bands[f // each][f % each]
+        filtered = lax.dot_general(inputs, band, LAST, preferred_element_type=jnp.float32)
         for b in range(blocks):
             filtered_ref[at : at + modes, b * HALF : (b + 1) * HALF] = filtered[8 * b : 8 * b + modes]
     columns = columns_ref[...]
@@ -145,11 +148,12 @@
         add_over_chunks(chunks, total, span, part, store)
 
 
-def edge_kernel(
-    chunks, halo_ref, filtered_ref, bands_ref, gain_ref, columns_ref, field_ref, out_hbm, wide, more, edge, total, sems
-):
+def edge_kernel(chunks, parts, halo_ref, filtered_ref, *refs):
+    bands, refs = refs[:parts], refs[parts:]
+    gain_ref, columns_ref, field_ref, out_hbm, wide, more, edge, total, sems = refs
     rows, steps = filtered_ref.shape
-    freqs = bands_ref.shape[0]
+    each = bands[0].shape[0]
+    freqs = parts * each
     modes = rows // freqs
     after = lax.axis_index("tm") == 0
     place = pl.multiple_of(jnp.where(after, steps - HALF, 0), HALF)
@@ -169,7 +173,11 @@
         at = f * modes
         inputs = jnp.concatenate([wide[i, at : at + 8, :] for i in range(2)], axis=1).astype(jnp.bfloat16)
         taps = jnp.concatenate(
-            [bands_ref[f, :, pl.ds(pl.multiple_of(reach + i * WINDOW, HALF), HALF)] for i in range(2)], axis=1
+            [
+                bands[f // each][f % each, :, pl.ds(pl.multiple_of(reach + i * WINDOW, HALF), HALF)]
+                for i in range(2)
+            ],
+            axis=1,
         )
         filtered = lax.dot_general(inputs, taps, LAST, preferred_element_type=jnp.float32)
         more[at : at + modes, :] = filtered[:modes]
@@ -190,10 +198,12 @@
 def band_field(coeffs, halo, bands, gain, columns):
     rows, steps = coeffs.shape
     dofs = columns.shape[1]
-    freqs = bands.shape[0]
+    freqs = sum(part.shape[0] for part in bands)
     chunk = min(CHUNK, freqs)
     chunks = freqs // chunk
     one = chunks == 1
+    bands = bands if one else [jnp.concatenate(bands)]
+    parts = len(bands)
     held = rows // chunks
     grid = () if one else (chunks,)
     made = pltpu.VMEM if one else jax.ShapeDtypeStruct
@@ -201,13 +211,13 @@
     def rows_of(width):
         return WHOLE if one else pl.BlockSpec((held, width), lambda i: (i, 0))
 
-    taps = WHOLE if one else pl.BlockSpec((chunk, HALF, 2 * WINDOW), lambda i: (i, 0, 0))
+    taps = [WHOLE if one else pl.BlockSpec((chunk, HALF, 2 * WINDOW), lambda i: (i, 0, 0))] * parts
     params = pltpu.CompilerParams(vmem_limit_bytes=24 << 20)
     filtered, field = pl.pallas_call(
-        functools.partial(own_kernel, chunks),
+        functools.partial(own_kernel, chunks, parts),
         grid=grid,
         out_shape=[made((rows, steps), jnp.float32), made((steps, dofs), jnp.bfloat16)],
-        in_specs=[rows_of(steps), taps, rows_of(HALF), rows_of(dofs)],
+        in_specs=[rows_of(steps), *taps, rows_of(HALF), rows_of(dofs)],
         out_specs=[rows_of(steps), WHOLE],
         scratch_shapes=[
             pltpu.VMEM((2, held + 8, steps + 2 * HALF), jnp.float32),
@@ -218,12 +228,12 @@
             flops=2 * rows * dofs * steps, bytes_accessed=2 * steps * dofs, transcendentals=0
         ),
         name="own_field",
-    )(coeffs, bands, gain, columns)
+    )(coeffs, *bands, gain, columns)
     return pl.pallas_call(
-        functools.partial(edge_kernel, chunks),
+        functools.partial(edge_kernel, chunks, parts),
         grid=grid,
         out_shape=jax.ShapeDtypeStruct((steps, dofs), jnp.bfloat16),
-        in_specs=[rows_of(HALF), rows_of(steps), taps, rows_of(HALF), rows_of(dofs), WHOLE],
+        in_specs=[rows_of(HALF), rows_of(steps), *taps, rows_of(HALF), rows_of(dofs), WHOLE],
         out_specs=pl.BlockSpec(memory_space=pl.ANY),
         scratch_shapes=[
             pltpu.VMEM((2, held + 8, HALF), jnp.float32),
@@ -237,7 +247,7 @@
             flops=2 * rows * dofs * HALF, bytes_accessed=2 * steps * dofs, transcendentals=0
         ),
         name="edge_field",
-    )(halo, filtered, bands, gain, columns, field)
+    )(halo, filtered, *bands, gain, columns, field)
 
 
 def message_scale(dofs, all_dofs):
@@ -245,32 +255,47 @@
     return 2.0 ** math.floor(math.log2(65504 / (dofs * snapshot * column)))
 
 
-def exchanged(values, axis, apart, scale):
-    count = lax.axis_size(axis)
+def received(message, masks, swap):
+    count, cores = lax.axis_size("space"), lax.axis_size("tm")
+    others = []
+    for mask in masks:
+        pairs = [
+            (place * cores + core, (place ^ mask) * cores + (core ^ swap))
+            for place in range(count)
+            for core in range(cores)
+        ]
+        others.append(lax.ppermute(message, ("space", "tm"), pairs))
+    return others
+
+
+def exchanged(values, masks, scale, swap):
     message = (values * scale).astype(jnp.float16)
-    other = lax.ppermute(message, axis, [(i, i ^ apart) for i in range(count)])
-    return values + other.astype(jnp.float32) * (1 / scale)
+    message, values = lax.optimization_barrier((message, values))
+    if swap:
+        values = lax.ppermute(values, "tm", [(0, 1), (1, 0)])
+    others = received(message, masks, swap)
+    more = sum(other.astype(jnp.float32) for other in others)
+    return values + more * (1 / scale)
 
 
 def per_device(snapshots, mode_columns, filter_taps, mode_gain):
     columns = mode_columns.T
     devices = lax.axis_size("space")
     dofs = columns.shape[1]
-    taps = padded_taps(filter_taps)
+    coeffs = coefficients(columns, snapshots)
+    coeffs = exchanged(coeffs, (1, 2, 3), message_scale(dofs, dofs * devices), 1)
     gain = jnp.broadcast_to(mode_gain[:, None], (mode_gain.shape[0], HALF))
-    coeffs = coefficients(columns, snapshots)
-    apart = 1
+    taps, gain = lax.optimization_barrier((padded_taps(filter_taps), gain))
+    bands = band_matrices(taps)
+    coeffs, bands = lax.optimization_barrier((coeffs, bands))
+    apart = 4
     while 2 * apart < devices:
-        if apart == 2:
-            coeffs, taps = lax.optimization_barrier((coeffs, taps))
-        coeffs = exchanged(coeffs, "space", apart, message_scale(dofs * apart, dofs * devices))
+        coeffs = exchanged(coeffs, (apart,), message_scale(dofs * apart, dofs * devices), 0)
         apart *= 2
-    bands = band_matrices(taps)
-    coeffs, bands, gain = lax.optimization_barrier((coeffs, bands, gain))
-    coeffs = exchanged(coeffs, "space", apart, message_scale(dofs * apart, dofs * devices))
+    coeffs = exchanged(coeffs, (apart,), message_scale(dofs * apart, dofs * devices), 1)
     edge = jnp.where(lax.axis_index("tm") == 0, coeffs[:, -HALF:], coeffs[:, :HALF])
     halo = lax.ppermute(edge.astype(jnp.bfloat16), "tm", [(0, 1), (1, 0)])
-    return band_field(coeffs, halo, bands, gain, columns)
+    return band_field(coeffs, halo, [bands], gain, columns)
 
 
 def solution(mesh):

time: 19 us -> 17.7 us (0.932)
  starting transfers between devices: 5.82 us -> 4.57 us
  local copies, waits for them, and re-layouts: 0.81 us -> 1.46 us
  waiting for transfers between devices: 7.48 us -> 6.91 us
    ppermute x1, starting transfers between devices: 4.19 us -> 0.46 us  [per_device(): halo = lax.ppermute(edge.astype(jnp.bfloat16), 'tm', [(0, 1), (1, 0)])]
    ppermute x3 -> x6, starting transfers between devices: 1.63 us -> 4.11 us  [the longest x4 3.64 us: received(): others.append(lax.ppermute(message, ('space', 'tm'), pairs))]
    broadcast_in_dim x1, local copies, waits for them, and re-layouts: 0.07 us -> 0.73 us  [per_device(): gain = jnp.broadcast_to(mode_gain[:, None], (mode_gain.shape[0], HALF))]
    ppermute x3 -> x6, waiting for transfers between devices: 7.47 us -> 6.91 us  [the longest x4 6.91 us: received(): others.append(lax.ppermute(message, ('space', 'tm'), pairs))]
  transfers between devices with their start and end apart: 4 -> 7, of which waited for: 3 -> 3; matrix products, arithmetic and copies ran while one was open for 4% -> 8% of each run, Pallas kernels for 8% -> 9%
where the time goes in v3:
time: 17.7 us; the launch traced here: 17.5 us
  waiting for transfers between devices  6.91 us (39%)
  starting transfers between devices  4.57 us (26%)
  Pallas kernels  4.38 us (25%)
  local copies, waits for them, and re-layouts  1.46 us (8%)
    ppermute x4, waiting for transfers between devices, received(): others.append(lax.ppermute(message, ('space', 'tm'), pairs))  6.91 us
    ppermute x4, starting transfers between devices, received(): others.append(lax.ppermute(message, ('space', 'tm'), pairs))  3.64 us
    pallas_call x1, Pallas kernels, coefficients(): pl.pallas_call(coefficient_kernel, out_shape=pltpu.VMEM((rows, steps), jn...  1.58 us
    pallas_call x1, Pallas kernels, band_field(): pl.pallas_call(functools.partial(edge_kernel, chunks, parts), grid=grid,...  1.23 us
    pallas_call x1, Pallas kernels, band_field(): pl.pallas_call(functools.partial(own_kernel, chunks, parts), grid=grid, o...  1.09 us
    reshape x1, local copies, waits for them, and re-layouts, padded_taps(): rows = filter_taps.astype(jnp.float32).reshape(freqs * parts, taps)  0.73 us
    broadcast_in_dim x1, local copies, waits for them, and re-layouts, per_device(): gain = jnp.broadcast_to(mode_gain[:, None], (mode_gain.shape[0], HALF))  0.73 us
    pallas_call x1, Pallas kernels, band_matrices(): pl.pallas_call(band_kernel, grid=() if one else (freqs // chunk,), out_sh...  0.47 us
  transfers between devices with their start and end apart: 7, of which 3 were waited for; matrix products, arithmetic and copies ran while one was open for 8% of the time, Pallas kernels for 9%

profile of v3, /device:TPU:25, one launch (start us, length us, event | category | flops | bytes accessed | tf_op | source)
XLA Modules:
  0.0 17.5 jit_solution(14373155010799964190)
XLA Ops:
  0.0 1.6 %coefficients.1 = f32[48,512]{1,0:T(8,128)S(1)} custom-call(bf16[48,1024]{1,0:T(8,128)(2,1)} %bitcast.1, bf16[512,1024]{1,0:T(8,128)(2,1)} %snapshots_hbm.1), custom_call_target="tpu_custom_call" | custom-call | flops 50331648 | bytes 1048576 | tf_op jit(solution)/shard_map/coefficients/pallas_call | solution.py:42
  1.6 0.0 copy-start
  1.6 1.7 %collective-permute-start.3 = (f16[48,512]{1,0:T(8,128)(2,1)S(1)}, f16[48,512]{1,0:T(8,128)(2,1)S(1)}, u32[]{:S(2)}, u32[]{:S(2)}) collective-permute-start(f16[48,512]{1,0:T(8,128)(2,1)S(1)} %multiply_convert_fusion.1), channel_id=1, source_target_pairs={{0,7},{1,6},{2,5},{3,4},{4,3},{5,2},{6,1},{7,0},{8,15},{9,14},{10,... | collective-permute-start | bytes 147464 | tf_op jit(solution)/shard_map/ppermute | solution.py:267
  3.3 1.0 %collective-permute-start.2 = (f16[48,512]{1,0:T(8,128)(2,1)S(1)}, f16[48,512]{1,0:T(8,128)(2,1)S(1)}, u32[]{:S(2)}, u32[]{:S(2)}) collective-permute-start(f16[48,512]{1,0:T(8,128)(2,1)S(1)} %multiply_convert_fusion.1), channel_id=1, source_target_pairs={{0,5},{1,4},{2,7},{3,6},{4,1},{5,0},{6,3},{7,2},{8,13},{9,12},{10,... | collective-permute-start | bytes 147464 | tf_op jit(solution)/shard_map/ppermute | solution.py:267
  4.4 0.8 %collective-permute-start.1 = (f16[48,512]{1,0:T(8,128)(2,1)S(1)}, f16[48,512]{1,0:T(8,128)(2,1)S(1)}, u32[]{:S(2)}, u32[]{:S(2)}) collective-permute-start(f16[48,512]{1,0:T(8,128)(2,1)S(1)} %multiply_convert_fusion.1), channel_id=1, source_target_pairs={{0,3},{1,2},{2,1},{3,0},{4,7},{5,6},{6,5},{7,4},{8,11},{9,10},{10,... | collective-permute-start | bytes 147464 | tf_op jit(solution)/shard_map/ppermute | solution.py:267
  5.2 0.0 collective-permute-start
  5.2 0.7 %reshape.5 = bf16[16,257]{1,0:T(8,128)(2,1)S(1)} reshape(bf16[8,2,257]{2,1,0:T(2,128)(2,1)} %param.6) | data formatting | bytes 16448 | tf_op jit(solution)/shard_map/reshape | solution.py:72
  5.9 0.7 %broadcast_in_dim.2.refs_1_ = f32[48,128]{1,0:T(8,128)S(1)} broadcast(f32[48]{0:T(128)} %param.7), dimensions={0} | broadcast | bytes 24768 | tf_op jit(solution)/shard_map/broadcast_in_dim | solution.py:287
  6.7 0.5 %band_matrices.1.refs_0_ = bf16[8,128,768]{2,1,0:T(8,128)(2,1)S(1)} custom-call(f32[16,384]{1,0:T(8,128)S(1)} %pad_convert_fusion.taps_ref), custom_call_target="tpu_custom_call" | custom-call | flops 15728640 | bytes 1572864 | tf_op jit(solution)/shard_map/band_matrices/pallas_call | solution.py:81
  7.1 0.0 collective-permute-done.3
  7.1 0.8 %collective-permute-done.2 = f16[48,512]{1,0:T(8,128)(2,1)S(1)} collective-permute-done((f16[48,512]{1,0:T(8,128)(2,1)S(1)}, f16[48,512]{1,0:T(8,128)(2,1)S(1)}, u32[]{:S(2)}, u32[]{:S(2)}) %collective-permute-start.2) | collective-permute-done | bytes 49184 | tf_op jit(solution)/shard_map/ppermute | solution.py:267
  8.0 0.7 %collective-permute-done.1 = f16[48,512]{1,0:T(8,128)(2,1)S(1)} collective-permute-done((f16[48,512]{1,0:T(8,128)(2,1)S(1)}, f16[48,512]{1,0:T(8,128)(2,1)S(1)}, u32[]{:S(2)}, u32[]{:S(2)}) %collective-permute-start.1) | collective-permute-done | bytes 49184 | tf_op jit(solution)/shard_map/ppermute | solution.py:267
  8.7 0.0 collective-permute-done
  8.7 0.5 %collective-permute-start.4 = (f32[48,512]{1,0:T(8,128)S(1)}, f32[48,512]{1,0:T(8,128)S(1)}, u32[]{:S(2)}, u32[]{:S(2)}) collective-permute-start(f32[48,512]{1,0:T(8,128)S(1)} %multiply_add_fusion.1), channel_id=1, source_target_pairs={{0,1},{1,0},{2,3},{3,2},{4,5},{5,4},{6,7},{7,6},{8,9},{9,8},{10,11... | collective-permute-start | bytes 294920 | tf_op jit(solution)/shard_map/ppermute | solution.py:275
  9.2 0.1 collective-permute-start.5
  9.3 5.4 %collective-permute-done.5 = f16[48,512]{1,0:T(8,128)(2,1)S(1)} collective-permute-done((f16[48,512]{1,0:T(8,128)(2,1)S(1)}, f16[48,512]{1,0:T(8,128)(2,1)S(1)}, u32[]{:S(2)}, u32[]{:S(2)}) %collective-permute-start.5) | collective-permute-done | bytes 49184 | tf_op jit(solution)/shard_map/ppermute | solution.py:267
  14.7 0.0 collective-permute-done.4
  14.7 0.5 %collective-permute-start.6 = (bf16[48,128]{1,0:T(8,128)(2,1)S(1)}, bf16[48,128]{1,0:T(8,128)(2,1)S(1)}, u32[]{:S(2)}, u32[]{:S(2)}) collective-permute-start(bf16[48,128]{1,0:T(8,128)(2,1)S(1)} %fusion), channel_id=1, source_target_pairs={{0,1},{1,0},{2,3},{3,2},{4,5},{5,4},{6,7},{7,6},{8,9},{9,8},{10,11... | collective-permute-start | bytes 36872 | tf_op jit(solution)/shard_map/ppermute | solution.py:297
  15.2 0.0 copy-done
  15.2 1.1 %own_field.1 = (f32[48,512]{1,0:T(8,128)S(1)}, bf16[512,1024]{1,0:T(8,128)(2,1)S(1)}) custom-call(f32[48,512]{1,0:T(8,128)S(1)} %multiply_add_fusion.coeffs_ref, bf16[8,128,768]{2,1,0:T(8,128)(2,1)S(1)} %band_matrices.1.refs_0_, f32[48,128]{1,0:T(8,128)S(1)} %broadcast_in_dim.2.refs_1_, bf16[48,1024]{1,0:T(8,128)(2,1)S(1)} %bitcast.2), custom_call_target="tpu_custom_call" | custom-call | flops 50331648 | bytes 1048576 | tf_op jit(solution)/shard_map/own_field/pallas_call | solution.py:216
  16.3 0.0 collective-permute-done.6.halo_ref
  16.3 1.2 %edge_field.1 = bf16[512,1024]{1,0:T(8,128)(2,1)} custom-call(bf16[48,128]{1,0:T(8,128)(2,1)S(1)} %collective-permute-done.6.halo_ref, f32[48,512]{1,0:T(8,128)S(1)} %get-tuple-element.23.filtered_ref, bf16[8,128,768]{2,1,0:T(8,128)(2,1)S(1)} %band_matrices.1.refs_0_, f32[48,128]{1,0:T(8,128)S(1)} %broadcast_in_dim.2.refs_1_, bf16[48,1024]{1,0:T(8,128)(2,1)S(1)} %bitcast.3, ...), custom_call_target="tpu_custom_call" | custom-call | flops 12582912 | bytes 1048576 | tf_op jit(solution)/shard_map/edge_field/pallas_call | solution.py:232
  (6 shorter events, 0.1 us)
Async XLA Ops:
  1.6 13.6 %copy-start = (bf16[1024,48]{0,1:T(8,128)(2,1)S(1)}, bf16[1024,48]{0,1:T(8,128)(2,1)}, u32[]{:S(2)}) copy-start(bf16[1024,48]{0,1:T(8,128)(2,1)} %param.5) | copy-start | bytes 294916
  1.6 5.5 %collective-permute-start.3 = (f16[48,512]{1,0:T(8,128)(2,1)S(1)}, f16[48,512]{1,0:T(8,128)(2,1)S(1)}, u32[]{:S(2)}, u32[]{:S(2)}) collective-permute-start(f16[48,512]{1,0:T(8,128)(2,1)S(1)} %multiply_convert_fusion.1), channel_id=1, source_target_pairs={{0,7},{1,6},{2,5},{3,4},{4,3},{5,2},{6,1},{7,0},{8,15},{9,14},{10,... | collective-permute-start | bytes 147464 | tf_op jit(solution)/shard_map/ppermute | solution.py:267
  3.3 4.6 %collective-permute-start.2 = (f16[48,512]{1,0:T(8,128)(2,1)S(1)}, f16[48,512]{1,0:T(8,128)(2,1)S(1)}, u32[]{:S(2)}, u32[]{:S(2)}) collective-permute-start(f16[48,512]{1,0:T(8,128)(2,1)S(1)} %multiply_convert_fusion.1), channel_id=1, source_target_pairs={{0,5},{1,4},{2,7},{3,6},{4,1},{5,0},{6,3},{7,2},{8,13},{9,12},{10,... | collective-permute-start | bytes 147464 | tf_op jit(solution)/shard_map/ppermute | solution.py:267
  4.4 4.3 %collective-permute-start.1 = (f16[48,512]{1,0:T(8,128)(2,1)S(1)}, f16[48,512]{1,0:T(8,128)(2,1)S(1)}, u32[]{:S(2)}, u32[]{:S(2)}) collective-permute-start(f16[48,512]{1,0:T(8,128)(2,1)S(1)} %multiply_convert_fusion.1), channel_id=1, source_target_pairs={{0,3},{1,2},{2,1},{3,0},{4,7},{5,6},{6,5},{7,4},{8,11},{9,10},{10,... | collective-permute-start | bytes 147464 | tf_op jit(solution)/shard_map/ppermute | solution.py:267
  5.2 3.5 %collective-permute-start = (f32[48,512]{1,0:T(8,128)S(1)}, f32[48,512]{1,0:T(8,128)S(1)}, u32[]{:S(2)}, u32[]{:S(2)}) collective-permute-start(f32[48,512]{1,0:T(8,128)S(1)} %coefficients.1), channel_id=1, source_target_pairs={{0,1},{1,0},{2,3},{3,2},{4,5},{5,4},{6,7},{7,6},{8,9},{9,8},{10,11... | collective-permute-start | bytes 294920 | tf_op jit(solution)/shard_map/ppermute | solution.py:275
  8.7 5.9 %collective-permute-start.4 = (f32[48,512]{1,0:T(8,128)S(1)}, f32[48,512]{1,0:T(8,128)S(1)}, u32[]{:S(2)}, u32[]{:S(2)}) collective-permute-start(f32[48,512]{1,0:T(8,128)S(1)} %multiply_add_fusion.1), channel_id=1, source_target_pairs={{0,1},{1,0},{2,3},{3,2},{4,5},{5,4},{6,7},{7,6},{8,9},{9,8},{10,11... | collective-permute-start | bytes 294920 | tf_op jit(solution)/shard_map/ppermute | solution.py:275
  9.2 5.5 %collective-permute-start.5 = (f16[48,512]{1,0:T(8,128)(2,1)S(1)}, f16[48,512]{1,0:T(8,128)(2,1)S(1)}, u32[]{:S(2)}, u32[]{:S(2)}) collective-permute-start(f16[48,512]{1,0:T(8,128)(2,1)S(1)} %multiply_convert_fusion), channel_id=1, source_target_pairs={{0,9},{1,8},{2,11},{3,10},{4,13},{5,12},{6,15},{7,14},{8,1},{9,0},... | collective-permute-start | bytes 147464 | tf_op jit(solution)/shard_map/ppermute | solution.py:267
  14.7 1.6 %collective-permute-start.6 = (bf16[48,128]{1,0:T(8,128)(2,1)S(1)}, bf16[48,128]{1,0:T(8,128)(2,1)S(1)}, u32[]{:S(2)}, u32[]{:S(2)}) collective-permute-start(bf16[48,128]{1,0:T(8,128)(2,1)S(1)} %fusion), channel_id=1, source_target_pairs={{0,1},{1,0},{2,3},{3,2},{4,5},{5,4},{6,7},{7,6},{8,9},{9,8},{10,11... | collective-permute-start | bytes 36872 | tf_op jit(solution)/shard_map/ppermute | solution.py:297

commit v4 on v3

--- a/solution.py
+++ b/solution.py
@@ -102,11 +102,17 @@
         store(part)
         return
     step = pl.program_id(0)
-    total[span, :] = jnp.where(step == 0, part, total[span, :] + part)
+    total[span] = jnp.where(step == 0, part, total[span] + part)
 
     @pl.when(step == chunks - 1)
     def _():
-        store(total[span, :])
+        store(total[span])
+
+
+def places(steps):
+    after = lax.axis_index("tm") == 0
+    rest = pl.multiple_of(jnp.where(after, 0, HALF), HALF)
+    return rest, pl.multiple_of(jnp.where(after, steps - HALF, 0), HALF)
 
 
 def own_kernel(chunks, parts, coeffs_ref, *refs):
@@ -137,15 +143,16 @@
         for b in range(blocks):
             filtered_ref[at : at + modes, b * HALF : (b + 1) * HALF] = filtered[8 * b : 8 * b + modes]
     columns = columns_ref[...]
-    for b in range(blocks):
-        span = slice(b * HALF, (b + 1) * HALF)
+    rest, _ = places(steps)
+    for b in range(blocks - 1):
+        span = pl.ds(pl.multiple_of(rest + b * HALF, HALF), HALF)
         piece = (filtered_ref[:, span] * gain_ref[...]).astype(jnp.bfloat16)
         part = lax.dot_general(piece, columns, FIRST, preferred_element_type=jnp.float32)
 
         def store(values, span=span):
             field_ref[span, :] = values.astype(jnp.bfloat16)
 
-        add_over_chunks(chunks, total, span, part, store)
+        add_over_chunks(chunks, total, (span, slice(None)), part, store)
 
 
 def edge_kernel(chunks, parts, halo_ref, filtered_ref, *refs):
@@ -155,14 +162,11 @@
     each = bands[0].shape[0]
     freqs = parts * each
     modes = rows // freqs
-    after = lax.axis_index("tm") == 0
-    place = pl.multiple_of(jnp.where(after, steps - HALF, 0), HALF)
-    rest = pl.multiple_of(jnp.where(after, 0, HALF), HALF)
-    reach = pl.multiple_of(jnp.where(after, WINDOW - HALF, 0), HALF)
+    rest, place = places(steps)
+    reach = pl.multiple_of(jnp.where(rest == 0, WINDOW - HALF, 0), HALF)
     first = pltpu.make_async_copy(
         field_ref.at[pl.ds(rest, steps - HALF)], out_hbm.at[pl.ds(rest, steps - HALF)], sems.at[0]
     )
-    last = pltpu.make_async_copy(edge, out_hbm.at[pl.ds(place, HALF)], sems.at[1])
     if chunks == 1:
         first.start()
     cells = halo_ref[...].astype(jnp.float32)
@@ -182,17 +186,30 @@
         filtered = lax.dot_general(inputs, taps, LAST, preferred_element_type=jnp.float32)
         more[at : at + modes, :] = filtered[:modes]
     piece = ((filtered_ref[:, pl.ds(place, HALF)] + more[...]) * gain_ref[...]).astype(jnp.bfloat16)
-    part = lax.dot_general(piece, columns_ref[...], FIRST, preferred_element_type=jnp.float32)
-
-    def store(values):
-        edge[...] = values.astype(jnp.bfloat16)
-        last.start()
+    width = columns_ref.shape[1] // SPLITS
+    copies = [first]
+    for i in range(SPLITS):
+        span = (slice(None), slice(i * width, (i + 1) * width))
+        part = lax.dot_general(piece, columns_ref[span], FIRST, preferred_element_type=jnp.float32)
+        target = out_hbm.at[pl.ds(place, HALF), pl.ds(i * width, width)]
+        copies.append(pltpu.make_async_copy(edge.at[span], target, sems.at[1 + i]))
+
+        def store(values, span=span, copy=copies[-1]):
+            edge[span] = values.astype(jnp.bfloat16)
+            copy.start()
+
+        add_over_chunks(chunks, total, span, part, store)
+
+    def finish():
         if chunks > 1:
             first.start()
-        first.wait()
-        last.wait()
-
-    add_over_chunks(chunks, total, slice(0, HALF), part, store)
+        for copy in copies:
+            copy.wait()
+
+    if chunks == 1:
+        finish()
+    else:
+        pl.when(pl.program_id(0) == chunks - 1)(finish)
 
 
 def band_field(coeffs, halo, bands, gain, columns):
@@ -240,7 +257,7 @@
             pltpu.VMEM((held, HALF), jnp.float32),
             pltpu.VMEM((HALF, dofs), jnp.bfloat16),
             pltpu.VMEM((8 if one else HALF, dofs), jnp.float32),
-            pltpu.SemaphoreType.DMA((2,)),
+            pltpu.SemaphoreType.DMA((1 + SPLITS,)),
         ],
         compiler_params=params,
         cost_estimate=pl.CostEstimate(
@@ -270,12 +287,10 @@
 
 def exchanged(values, masks, scale, swap):
     message = (values * scale).astype(jnp.float16)
-    message, values = lax.optimization_barrier((message, values))
-    if swap:
-        values = lax.ppermute(values, "tm", [(0, 1), (1, 0)])
-    others = received(message, masks, swap)
-    more = sum(other.astype(jnp.float32) for other in others)
-    return values + more * (1 / scale)
+    others = [lax.ppermute(message, "tm", [(0, 1), (1, 0)])] if swap else []
+    others += received(message, masks, swap)
+    more = sum(other.astype(jnp.float32) for other in others) * (1 / scale)
+    return more if swap else values + more
 
 
 def per_device(snapshots, mode_columns, filter_taps, mode_gain):

time: 17.7 us -> 17.5 us (0.989)
    ppermute x2, starting transfers between devices: 0.46 us -> 0.14 us  [exchanged(): others = [lax.ppermute(message, 'tm', [(0, 1), (1, 0)])] if swap else []]
    ppermute x4, starting transfers between devices: 3.64 us -> 3.95 us  [received(): others.append(lax.ppermute(message, ('space', 'tm'), pairs))]
where the time goes in v4:
time: 17.5 us; the launch traced here: 17.3 us
  waiting for transfers between devices  6.8 us (39%)
  starting transfers between devices  4.55 us (26%)
  Pallas kernels  4.32 us (25%)
  local copies, waits for them, and re-layouts  1.46 us (8%)
    ppermute x4, waiting for transfers between devices, received(): others.append(lax.ppermute(message, ('space', 'tm'), pairs))  6.79 us
    ppermute x4, starting transfers between devices, received(): others.append(lax.ppermute(message, ('space', 'tm'), pairs))  3.95 us
    pallas_call x1, Pallas kernels, coefficients(): pl.pallas_call(coefficient_kernel, out_shape=pltpu.VMEM((rows, steps), jn...  1.61 us
    pallas_call x1, Pallas kernels, band_field(): pl.pallas_call(functools.partial(edge_kernel, chunks, parts), grid=grid,...  1.21 us
    pallas_call x1, Pallas kernels, band_field(): pl.pallas_call(functools.partial(own_kernel, chunks, parts), grid=grid, o...  1.01 us
    reshape x1, local copies, waits for them, and re-layouts, padded_taps(): rows = filter_taps.astype(jnp.float32).reshape(freqs * parts, taps)  0.73 us
    broadcast_in_dim x1, local copies, waits for them, and re-layouts, per_device(): gain = jnp.broadcast_to(mode_gain[:, None], (mode_gain.shape[0], HALF))  0.73 us
    pallas_call x1, Pallas kernels, band_matrices(): pl.pallas_call(band_kernel, grid=() if one else (freqs // chunk,), out_sh...  0.47 us
  transfers between devices with their start and end apart: 7, of which 3 were waited for; matrix products, arithmetic and copies ran while one was open for 8% of the time, Pallas kernels for 9%

profile of v4, /device:TPU:25, one launch (start us, length us, event | category | flops | bytes accessed | tf_op | source)
XLA Modules:
  0.0 17.3 jit_solution(15491093362370226431)
XLA Ops:
  0.0 0.0 copy-start
  0.0 1.6 %coefficients.1 = f32[48,512]{1,0:T(8,128)S(1)} custom-call(bf16[48,1024]{1,0:T(8,128)(2,1)} %bitcast.1, bf16[512,1024]{1,0:T(8,128)(2,1)} %snapshots_hbm.1), custom_call_target="tpu_custom_call" | custom-call | flops 50331648 | bytes 1048576 | tf_op jit(solution)/shard_map/coefficients/pallas_call | solution.py:42
  1.6 1.7 %collective-permute-start.3 = (f16[48,512]{1,0:T(8,128)(2,1)S(1)}, f16[48,512]{1,0:T(8,128)(2,1)S(1)}, u32[]{:S(2)}, u32[]{:S(2)}) collective-permute-start(f16[48,512]{1,0:T(8,128)(2,1)S(1)} %multiply_convert_fusion.1), channel_id=1, source_target_pairs={{0,7},{1,6},{2,5},{3,4},{4,3},{5,2},{6,1},{7,0},{8,15},{9,14},{10,... | collective-permute-start | bytes 147464 | tf_op jit(solution)/shard_map/ppermute | solution.py:284
  3.4 1.0 %collective-permute-start.2 = (f16[48,512]{1,0:T(8,128)(2,1)S(1)}, f16[48,512]{1,0:T(8,128)(2,1)S(1)}, u32[]{:S(2)}, u32[]{:S(2)}) collective-permute-start(f16[48,512]{1,0:T(8,128)(2,1)S(1)} %multiply_convert_fusion.1), channel_id=1, source_target_pairs={{0,5},{1,4},{2,7},{3,6},{4,1},{5,0},{6,3},{7,2},{8,13},{9,12},{10,... | collective-permute-start | bytes 147464 | tf_op jit(solution)/shard_map/ppermute | solution.py:284
  4.4 0.8 %collective-permute-start.1 = (f16[48,512]{1,0:T(8,128)(2,1)S(1)}, f16[48,512]{1,0:T(8,128)(2,1)S(1)}, u32[]{:S(2)}, u32[]{:S(2)}) collective-permute-start(f16[48,512]{1,0:T(8,128)(2,1)S(1)} %multiply_convert_fusion.1), channel_id=1, source_target_pairs={{0,3},{1,2},{2,1},{3,0},{4,7},{5,6},{6,5},{7,4},{8,11},{9,10},{10,... | collective-permute-start | bytes 147464 | tf_op jit(solution)/shard_map/ppermute | solution.py:284
  5.2 0.0 collective-permute-start
  5.2 0.7 %reshape.5 = bf16[16,257]{1,0:T(8,128)(2,1)S(1)} reshape(bf16[8,2,257]{2,1,0:T(2,128)(2,1)} %param.6) | data formatting | bytes 16448 | tf_op jit(solution)/shard_map/reshape | solution.py:72
  5.9 0.7 %broadcast_in_dim.2.refs_1_ = f32[48,128]{1,0:T(8,128)S(1)} broadcast(f32[48]{0:T(128)} %param.7), dimensions={0} | broadcast | bytes 24768 | tf_op jit(solution)/shard_map/broadcast_in_dim | solution.py:302
  6.7 0.5 %band_matrices.1.refs_0_ = bf16[8,128,768]{2,1,0:T(8,128)(2,1)S(1)} custom-call(f32[16,384]{1,0:T(8,128)S(1)} %pad_convert_fusion.taps_ref), custom_call_target="tpu_custom_call" | custom-call | flops 15728640 | bytes 1572864 | tf_op jit(solution)/shard_map/band_matrices/pallas_call | solution.py:81
  7.2 0.0 collective-permute-done.3
  7.2 0.8 %collective-permute-done.2 = f16[48,512]{1,0:T(8,128)(2,1)S(1)} collective-permute-done((f16[48,512]{1,0:T(8,128)(2,1)S(1)}, f16[48,512]{1,0:T(8,128)(2,1)S(1)}, u32[]{:S(2)}, u32[]{:S(2)}) %collective-permute-start.2) | collective-permute-done | bytes 49184 | tf_op jit(solution)/shard_map/ppermute | solution.py:284
  8.0 0.7 %collective-permute-done.1 = f16[48,512]{1,0:T(8,128)(2,1)S(1)} collective-permute-done((f16[48,512]{1,0:T(8,128)(2,1)S(1)}, f16[48,512]{1,0:T(8,128)(2,1)S(1)}, u32[]{:S(2)}, u32[]{:S(2)}) %collective-permute-start.1) | collective-permute-done | bytes 49184 | tf_op jit(solution)/shard_map/ppermute | solution.py:284
  8.7 0.0 collective-permute-done
  8.7 0.4 %collective-permute-start.5 = (f16[48,512]{1,0:T(8,128)(2,1)S(1)}, f16[48,512]{1,0:T(8,128)(2,1)S(1)}, u32[]{:S(2)}, u32[]{:S(2)}) collective-permute-start(f16[48,512]{1,0:T(8,128)(2,1)S(1)} %multiply_convert_fusion), channel_id=1, source_target_pairs={{0,9},{1,8},{2,11},{3,10},{4,13},{5,12},{6,15},{7,14},{8,1},{9,0},... | collective-permute-start | bytes 147464 | tf_op jit(solution)/shard_map/ppermute | solution.py:284
  9.1 0.1 collective-permute-start.4
  9.3 5.3 %collective-permute-done.5 = f16[48,512]{1,0:T(8,128)(2,1)S(1)} collective-permute-done((f16[48,512]{1,0:T(8,128)(2,1)S(1)}, f16[48,512]{1,0:T(8,128)(2,1)S(1)}, u32[]{:S(2)}, u32[]{:S(2)}) %collective-permute-start.5) | collective-permute-done | bytes 49184 | tf_op jit(solution)/shard_map/ppermute | solution.py:284
  14.5 0.0 collective-permute-done.4
  14.6 0.5 %collective-permute-start.6 = (bf16[48,128]{1,0:T(8,128)(2,1)S(1)}, bf16[48,128]{1,0:T(8,128)(2,1)S(1)}, u32[]{:S(2)}, u32[]{:S(2)}) collective-permute-start(bf16[48,128]{1,0:T(8,128)(2,1)S(1)} %fusion), channel_id=1, source_target_pairs={{0,1},{1,0},{2,3},{3,2},{4,5},{5,4},{6,7},{7,6},{8,9},{9,8},{10,11... | collective-permute-start | bytes 36872 | tf_op jit(solution)/shard_map/ppermute | solution.py:312
  15.1 0.0 copy-done
  15.1 1.0 %own_field.1 = (f32[48,512]{1,0:T(8,128)S(1)}, bf16[512,1024]{1,0:T(8,128)(2,1)S(1)}) custom-call(f32[48,512]{1,0:T(8,128)S(1)} %add_multiply_fusion.coeffs_ref, bf16[8,128,768]{2,1,0:T(8,128)(2,1)S(1)} %band_matrices.1.refs_0_, f32[48,128]{1,0:T(8,128)S(1)} %broadcast_in_dim.2.refs_1_, bf16[48,1024]{1,0:T(8,128)(2,1)S(1)} %bitcast.2), custom_call_target="tpu_custom_call" | custom-call | flops 50331648 | bytes 1048576 | tf_op jit(solution)/shard_map/own_field/pallas_call | solution.py:233
  16.1 0.0 collective-permute-done.6.halo_ref
  16.1 1.2 %edge_field.1 = bf16[512,1024]{1,0:T(8,128)(2,1)} custom-call(bf16[48,128]{1,0:T(8,128)(2,1)S(1)} %collective-permute-done.6.halo_ref, f32[48,512]{1,0:T(8,128)S(1)} %get-tuple-element.15.filtered_ref, bf16[8,128,768]{2,1,0:T(8,128)(2,1)S(1)} %band_matrices.1.refs_0_, f32[48,128]{1,0:T(8,128)S(1)} %broadcast_in_dim.2.refs_1_, bf16[48,1024]{1,0:T(8,128)(2,1)S(1)} %bitcast.3, ...), custom_call_target="tpu_custom_call" | custom-call | flops 12582912 | bytes 1048576 | tf_op jit(solution)/shard_map/edge_field/pallas_call | solution.py:249
  (6 shorter events, 0.1 us)
Async XLA Ops:
  0.0 15.1 %copy-start = (bf16[1024,48]{0,1:T(8,128)(2,1)S(1)}, bf16[1024,48]{0,1:T(8,128)(2,1)}, u32[]{:S(2)}) copy-start(bf16[1024,48]{0,1:T(8,128)(2,1)} %param.5) | copy-start | bytes 294916
  1.6 5.5 %collective-permute-start.3 = (f16[48,512]{1,0:T(8,128)(2,1)S(1)}, f16[48,512]{1,0:T(8,128)(2,1)S(1)}, u32[]{:S(2)}, u32[]{:S(2)}) collective-permute-start(f16[48,512]{1,0:T(8,128)(2,1)S(1)} %multiply_convert_fusion.1), channel_id=1, source_target_pairs={{0,7},{1,6},{2,5},{3,4},{4,3},{5,2},{6,1},{7,0},{8,15},{9,14},{10,... | collective-permute-start | bytes 147464 | tf_op jit(solution)/shard_map/ppermute | solution.py:284
  3.4 4.6 %collective-permute-start.2 = (f16[48,512]{1,0:T(8,128)(2,1)S(1)}, f16[48,512]{1,0:T(8,128)(2,1)S(1)}, u32[]{:S(2)}, u32[]{:S(2)}) collective-permute-start(f16[48,512]{1,0:T(8,128)(2,1)S(1)} %multiply_convert_fusion.1), channel_id=1, source_target_pairs={{0,5},{1,4},{2,7},{3,6},{4,1},{5,0},{6,3},{7,2},{8,13},{9,12},{10,... | collective-permute-start | bytes 147464 | tf_op jit(solution)/shard_map/ppermute | solution.py:284
  4.4 4.3 %collective-permute-start.1 = (f16[48,512]{1,0:T(8,128)(2,1)S(1)}, f16[48,512]{1,0:T(8,128)(2,1)S(1)}, u32[]{:S(2)}, u32[]{:S(2)}) collective-permute-start(f16[48,512]{1,0:T(8,128)(2,1)S(1)} %multiply_convert_fusion.1), channel_id=1, source_target_pairs={{0,3},{1,2},{2,1},{3,0},{4,7},{5,6},{6,5},{7,4},{8,11},{9,10},{10,... | collective-permute-start | bytes 147464 | tf_op jit(solution)/shard_map/ppermute | solution.py:284
  5.2 3.5 %collective-permute-start = (f16[48,512]{1,0:T(8,128)(2,1)S(1)}, f16[48,512]{1,0:T(8,128)(2,1)S(1)}, u32[]{:S(2)}, u32[]{:S(2)}) collective-permute-start(f16[48,512]{1,0:T(8,128)(2,1)S(1)} %multiply_convert_fusion.1), channel_id=1, source_target_pairs={{0,1},{1,0},{2,3},{3,2},{4,5},{5,4},{6,7},{7,6},{8,9},{9,8},{10,11... | collective-permute-start | bytes 147464 | tf_op jit(solution)/shard_map/ppermute | solution.py:290
  8.7 5.8 %collective-permute-start.5 = (f16[48,512]{1,0:T(8,128)(2,1)S(1)}, f16[48,512]{1,0:T(8,128)(2,1)S(1)}, u32[]{:S(2)}, u32[]{:S(2)}) collective-permute-start(f16[48,512]{1,0:T(8,128)(2,1)S(1)} %multiply_convert_fusion), channel_id=1, source_target_pairs={{0,9},{1,8},{2,11},{3,10},{4,13},{5,12},{6,15},{7,14},{8,1},{9,0},... | collective-permute-start | bytes 147464 | tf_op jit(solution)/shard_map/ppermute | solution.py:284
  9.1 5.4 %collective-permute-start.4 = (f16[48,512]{1,0:T(8,128)(2,1)S(1)}, f16[48,512]{1,0:T(8,128)(2,1)S(1)}, u32[]{:S(2)}, u32[]{:S(2)}) collective-permute-start(f16[48,512]{1,0:T(8,128)(2,1)S(1)} %multiply_convert_fusion), channel_id=1, source_target_pairs={{0,1},{1,0},{2,3},{3,2},{4,5},{5,4},{6,7},{7,6},{8,9},{9,8},{10,11... | collective-permute-start | bytes 147464 | tf_op jit(solution)/shard_map/ppermute | solution.py:290
  14.6 1.5 %collective-permute-start.6 = (bf16[48,128]{1,0:T(8,128)(2,1)S(1)}, bf16[48,128]{1,0:T(8,128)(2,1)S(1)}, u32[]{:S(2)}, u32[]{:S(2)}) collective-permute-start(bf16[48,128]{1,0:T(8,128)(2,1)S(1)} %fusion), channel_id=1, source_target_pairs={{0,1},{1,0},{2,3},{3,2},{4,5},{5,4},{6,7},{7,6},{8,9},{9,8},{10,11... | collective-permute-start | bytes 36872 | tf_op jit(solution)/shard_map/ppermute | solution.py:312

commit v5 on v4

--- a/solution.py
+++ b/solution.py
@@ -285,12 +285,15 @@
     return others
 
 
-def exchanged(values, masks, scale, swap):
+def exchanged(values, masks, scale, swap, ready=None):
     message = (values * scale).astype(jnp.float16)
+    if ready is not None:
+        message, ready = lax.optimization_barrier((message, ready))
     others = [lax.ppermute(message, "tm", [(0, 1), (1, 0)])] if swap else []
     others += received(message, masks, swap)
     more = sum(other.astype(jnp.float32) for other in others) * (1 / scale)
-    return more if swap else values + more
+    values = more if swap else values + more
+    return values if ready is None else (values, ready)
 
 
 def per_device(snapshots, mode_columns, filter_taps, mode_gain):
@@ -298,16 +301,15 @@
     devices = lax.axis_size("space")
     dofs = columns.shape[1]
     coeffs = coefficients(columns, snapshots)
-    coeffs = exchanged(coeffs, (1, 2, 3), message_scale(dofs, dofs * devices), 1)
+    coeffs = exchanged(coeffs, (4,), message_scale(dofs, dofs * devices), 1)
     gain = jnp.broadcast_to(mode_gain[:, None], (mode_gain.shape[0], HALF))
     taps, gain = lax.optimization_barrier((padded_taps(filter_taps), gain))
     bands = band_matrices(taps)
-    coeffs, bands = lax.optimization_barrier((coeffs, bands))
-    apart = 4
-    while 2 * apart < devices:
-        coeffs = exchanged(coeffs, (apart,), message_scale(dofs * apart, dofs * devices), 0)
+    apart = 8
+    while apart < devices:
+        coeffs = exchanged(coeffs, (apart,), message_scale(dofs * apart // 4, dofs * devices), 0)
         apart *= 2
-    coeffs = exchanged(coeffs, (apart,), message_scale(dofs * apart, dofs * devices), 1)
+    coeffs, bands = exchanged(coeffs, (1, 2, 3), message_scale(dofs * devices // 4, dofs * devices), 1, bands)
     edge = jnp.where(lax.axis_index("tm") == 0, coeffs[:, -HALF:], coeffs[:, :HALF])
     halo = lax.ppermute(edge.astype(jnp.bfloat16), "tm", [(0, 1), (1, 0)])
     return band_field(coeffs, halo, [bands], gain, columns)

time: 17.5 us -> 17.4 us (level)
  waiting for transfers between devices: 6.8 us -> 6.62 us
    ppermute x4, waiting for transfers between devices: 6.79 us -> 6.61 us  [received(): others.append(lax.ppermute(message, ('space', 'tm'), pairs))]
  transfers between devices with their start and end apart: 7 -> 7, of which waited for: 3 -> 4; matrix products, arithmetic and copies ran while one was open for 8% -> 9% of each run, Pallas kernels for 9% -> 9%
where the time goes in v5:
time: 17.4 us; the launch traced here: 17.2 us
  waiting for transfers between devices  6.62 us (38%)
  starting transfers between devices  4.67 us (27%)
  Pallas kernels  4.31 us (25%)
  local copies, waits for them, and re-layouts  1.46 us (8%)
    ppermute x4, waiting for transfers between devices, received(): others.append(lax.ppermute(message, ('space', 'tm'), pairs))  6.61 us
    ppermute x4, starting transfers between devices, received(): others.append(lax.ppermute(message, ('space', 'tm'), pairs))  3.99 us
    pallas_call x1, Pallas kernels, coefficients(): pl.pallas_call(coefficient_kernel, out_shape=pltpu.VMEM((rows, steps), jn...  1.61 us
    pallas_call x1, Pallas kernels, band_field(): pl.pallas_call(functools.partial(edge_kernel, chunks, parts), grid=grid,...  1.21 us
    pallas_call x1, Pallas kernels, band_field(): pl.pallas_call(functools.partial(own_kernel, chunks, parts), grid=grid, o...  1.01 us
    reshape x1, local copies, waits for them, and re-layouts, padded_taps(): rows = filter_taps.astype(jnp.float32).reshape(freqs * parts, taps)  0.73 us
    broadcast_in_dim x1, local copies, waits for them, and re-layouts, per_device(): gain = jnp.broadcast_to(mode_gain[:, None], (mode_gain.shape[0], HALF))  0.73 us
    pallas_call x1, Pallas kernels, band_matrices(): pl.pallas_call(band_kernel, grid=() if one else (freqs // chunk,), out_sh...  0.47 us
  transfers between devices with their start and end apart: 7, of which 4 were waited for; matrix products, arithmetic and copies ran while one was open for 9% of the time, Pallas kernels for 9%

profile of v5, /device:TPU:25, one launch (start us, length us, event | category | flops | bytes accessed | tf_op | source)
XLA Modules:
  0.0 17.2 jit_solution(3120230268950180211)
XLA Ops:
  0.0 0.0 copy-start
  0.0 1.6 %coefficients.1 = f32[48,512]{1,0:T(8,128)S(1)} custom-call(bf16[48,1024]{1,0:T(8,128)(2,1)} %bitcast.1, bf16[512,1024]{1,0:T(8,128)(2,1)} %snapshots_hbm.1), custom_call_target="tpu_custom_call" | custom-call | flops 50331648 | bytes 1048576 | tf_op jit(solution)/shard_map/coefficients/pallas_call | solution.py:42
  1.6 0.7 %collective-permute-start.1 = (f16[48,512]{1,0:T(8,128)(2,1)S(1)}, f16[48,512]{1,0:T(8,128)(2,1)S(1)}, u32[]{:S(2)}, u32[]{:S(2)}) collective-permute-start(f16[48,512]{1,0:T(8,128)(2,1)S(1)} %multiply_convert_fusion.1), channel_id=1, source_target_pairs={{0,9},{1,8},{2,11},{3,10},{4,13},{5,12},{6,15},{7,14},{8,1},{9,0},... | collective-permute-start | bytes 147464 | tf_op jit(solution)/shard_map/ppermute | solution.py:284
  2.3 0.1 collective-permute-start
  2.5 0.7 %reshape.5 = bf16[16,257]{1,0:T(8,128)(2,1)S(1)} reshape(bf16[8,2,257]{2,1,0:T(2,128)(2,1)} %param.6) | data formatting | bytes 16448 | tf_op jit(solution)/shard_map/reshape | solution.py:72
  3.2 0.7 %broadcast_in_dim.2.refs_1_ = f32[48,128]{1,0:T(8,128)S(1)} broadcast(f32[48]{0:T(128)} %param.7), dimensions={0} | broadcast | bytes 24768 | tf_op jit(solution)/shard_map/broadcast_in_dim | solution.py:305
  3.9 0.5 %band_matrices.1.refs_0_ = bf16[8,128,768]{2,1,0:T(8,128)(2,1)S(1)} custom-call(f32[16,384]{1,0:T(8,128)S(1)} %pad_convert_fusion.taps_ref), custom_call_target="tpu_custom_call" | custom-call | flops 15728640 | bytes 1572864 | tf_op jit(solution)/shard_map/band_matrices/pallas_call | solution.py:81
  4.4 3.4 %collective-permute-done.1 = f16[48,512]{1,0:T(8,128)(2,1)S(1)} collective-permute-done((f16[48,512]{1,0:T(8,128)(2,1)S(1)}, f16[48,512]{1,0:T(8,128)(2,1)S(1)}, u32[]{:S(2)}, u32[]{:S(2)}) %collective-permute-start.1) | collective-permute-done | bytes 49184 | tf_op jit(solution)/shard_map/ppermute | solution.py:284
  7.9 0.0 collective-permute-done
  7.9 0.6 %collective-permute-start.5 = (f16[48,512]{1,0:T(8,128)(2,1)S(1)}, f16[48,512]{1,0:T(8,128)(2,1)S(1)}, u32[]{:S(2)}, u32[]{:S(2)}) collective-permute-start(f16[48,512]{1,0:T(8,128)(2,1)S(1)} %multiply_convert_fusion), channel_id=1, source_target_pairs={{0,7},{1,6},{2,5},{3,4},{4,3},{5,2},{6,1},{7,0},{8,15},{9,14},{10,... | collective-permute-start | bytes 147464 | tf_op jit(solution)/shard_map/ppermute | solution.py:284
  8.5 2.1 %collective-permute-start.4 = (f16[48,512]{1,0:T(8,128)(2,1)S(1)}, f16[48,512]{1,0:T(8,128)(2,1)S(1)}, u32[]{:S(2)}, u32[]{:S(2)}) collective-permute-start(f16[48,512]{1,0:T(8,128)(2,1)S(1)} %multiply_convert_fusion), channel_id=1, source_target_pairs={{0,5},{1,4},{2,7},{3,6},{4,1},{5,0},{6,3},{7,2},{8,13},{9,12},{10,... | collective-permute-start | bytes 147464 | tf_op jit(solution)/shard_map/ppermute | solution.py:284
  10.6 0.6 %collective-permute-start.3 = (f16[48,512]{1,0:T(8,128)(2,1)S(1)}, f16[48,512]{1,0:T(8,128)(2,1)S(1)}, u32[]{:S(2)}, u32[]{:S(2)}) collective-permute-start(f16[48,512]{1,0:T(8,128)(2,1)S(1)} %multiply_convert_fusion), channel_id=1, source_target_pairs={{0,3},{1,2},{2,1},{3,0},{4,7},{5,6},{6,5},{7,4},{8,11},{9,10},{10,... | collective-permute-start | bytes 147464 | tf_op jit(solution)/shard_map/ppermute | solution.py:284
  11.2 0.1 collective-permute-start.2
  11.3 1.6 %collective-permute-done.5 = f16[48,512]{1,0:T(8,128)(2,1)S(1)} collective-permute-done((f16[48,512]{1,0:T(8,128)(2,1)S(1)}, f16[48,512]{1,0:T(8,128)(2,1)S(1)}, u32[]{:S(2)}, u32[]{:S(2)}) %collective-permute-start.5) | collective-permute-done | bytes 49184 | tf_op jit(solution)/shard_map/ppermute | solution.py:284
  12.9 1.1 %collective-permute-done.4 = f16[48,512]{1,0:T(8,128)(2,1)S(1)} collective-permute-done((f16[48,512]{1,0:T(8,128)(2,1)S(1)}, f16[48,512]{1,0:T(8,128)(2,1)S(1)}, u32[]{:S(2)}, u32[]{:S(2)}) %collective-permute-start.4) | collective-permute-done | bytes 49184 | tf_op jit(solution)/shard_map/ppermute | solution.py:284
  14.0 0.5 %collective-permute-done.3 = f16[48,512]{1,0:T(8,128)(2,1)S(1)} collective-permute-done((f16[48,512]{1,0:T(8,128)(2,1)S(1)}, f16[48,512]{1,0:T(8,128)(2,1)S(1)}, u32[]{:S(2)}, u32[]{:S(2)}) %collective-permute-start.3) | collective-permute-done | bytes 49184 | tf_op jit(solution)/shard_map/ppermute | solution.py:284
  14.4 0.0 collective-permute-done.2
  14.5 0.5 %collective-permute-start.6 = (bf16[48,128]{1,0:T(8,128)(2,1)S(1)}, bf16[48,128]{1,0:T(8,128)(2,1)S(1)}, u32[]{:S(2)}, u32[]{:S(2)}) collective-permute-start(bf16[48,128]{1,0:T(8,128)(2,1)S(1)} %fusion), channel_id=1, source_target_pairs={{0,1},{1,0},{2,3},{3,2},{4,5},{5,4},{6,7},{7,6},{8,9},{9,8},{10,11... | collective-permute-start | bytes 36872 | tf_op jit(solution)/shard_map/ppermute | solution.py:314
  15.0 0.0 copy-done
  15.0 1.0 %own_field.1 = (f32[48,512]{1,0:T(8,128)S(1)}, bf16[512,1024]{1,0:T(8,128)(2,1)S(1)}) custom-call(f32[48,512]{1,0:T(8,128)S(1)} %add_multiply_fusion.coeffs_ref, bf16[8,128,768]{2,1,0:T(8,128)(2,1)S(1)} %band_matrices.1.refs_0_, f32[48,128]{1,0:T(8,128)S(1)} %broadcast_in_dim.2.refs_1_, bf16[48,1024]{1,0:T(8,128)(2,1)S(1)} %bitcast.2), custom_call_target="tpu_custom_call" | custom-call | flops 50331648 | bytes 1048576 | tf_op jit(solution)/shard_map/own_field/pallas_call | solution.py:233
  16.0 0.0 collective-permute-done.6.halo_ref
  16.0 1.2 %edge_field.1 = bf16[512,1024]{1,0:T(8,128)(2,1)} custom-call(bf16[48,128]{1,0:T(8,128)(2,1)S(1)} %collective-permute-done.6.halo_ref, f32[48,512]{1,0:T(8,128)S(1)} %get-tuple-element.15.filtered_ref, bf16[8,128,768]{2,1,0:T(8,128)(2,1)S(1)} %band_matrices.1.refs_0_, f32[48,128]{1,0:T(8,128)S(1)} %broadcast_in_dim.2.refs_1_, bf16[48,1024]{1,0:T(8,128)(2,1)S(1)} %bitcast.3, ...), custom_call_target="tpu_custom_call" | custom-call | flops 12582912 | bytes 1048576 | tf_op jit(solution)/shard_map/edge_field/pallas_call | solution.py:249
  (5 shorter events, 0.1 us)
Async XLA Ops:
  0.0 15.0 %copy-start = (bf16[1024,48]{0,1:T(8,128)(2,1)S(1)}, bf16[1024,48]{0,1:T(8,128)(2,1)}, u32[]{:S(2)}) copy-start(bf16[1024,48]{0,1:T(8,128)(2,1)} %param.5) | copy-start | bytes 294916
  1.6 6.2 %collective-permute-start.1 = (f16[48,512]{1,0:T(8,128)(2,1)S(1)}, f16[48,512]{1,0:T(8,128)(2,1)S(1)}, u32[]{:S(2)}, u32[]{:S(2)}) collective-permute-start(f16[48,512]{1,0:T(8,128)(2,1)S(1)} %multiply_convert_fusion.1), channel_id=1, source_target_pairs={{0,9},{1,8},{2,11},{3,10},{4,13},{5,12},{6,15},{7,14},{8,1},{9,0},... | collective-permute-start | bytes 147464 | tf_op jit(solution)/shard_map/ppermute | solution.py:284
  2.3 5.5 %collective-permute-start = (f16[48,512]{1,0:T(8,128)(2,1)S(1)}, f16[48,512]{1,0:T(8,128)(2,1)S(1)}, u32[]{:S(2)}, u32[]{:S(2)}) collective-permute-start(f16[48,512]{1,0:T(8,128)(2,1)S(1)} %multiply_convert_fusion.1), channel_id=1, source_target_pairs={{0,1},{1,0},{2,3},{3,2},{4,5},{5,4},{6,7},{7,6},{8,9},{9,8},{10,11... | collective-permute-start | bytes 147464 | tf_op jit(solution)/shard_map/ppermute | solution.py:292
  7.9 5.0 %collective-permute-start.5 = (f16[48,512]{1,0:T(8,128)(2,1)S(1)}, f16[48,512]{1,0:T(8,128)(2,1)S(1)}, u32[]{:S(2)}, u32[]{:S(2)}) collective-permute-start(f16[48,512]{1,0:T(8,128)(2,1)S(1)} %multiply_convert_fusion), channel_id=1, source_target_pairs={{0,7},{1,6},{2,5},{3,4},{4,3},{5,2},{6,1},{7,0},{8,15},{9,14},{10,... | collective-permute-start | bytes 147464 | tf_op jit(solution)/shard_map/ppermute | solution.py:284
  8.5 5.5 %collective-permute-start.4 = (f16[48,512]{1,0:T(8,128)(2,1)S(1)}, f16[48,512]{1,0:T(8,128)(2,1)S(1)}, u32[]{:S(2)}, u32[]{:S(2)}) collective-permute-start(f16[48,512]{1,0:T(8,128)(2,1)S(1)} %multiply_convert_fusion), channel_id=1, source_target_pairs={{0,5},{1,4},{2,7},{3,6},{4,1},{5,0},{6,3},{7,2},{8,13},{9,12},{10,... | collective-permute-start | bytes 147464 | tf_op jit(solution)/shard_map/ppermute | solution.py:284
  10.6 3.8 %collective-permute-start.3 = (f16[48,512]{1,0:T(8,128)(2,1)S(1)}, f16[48,512]{1,0:T(8,128)(2,1)S(1)}, u32[]{:S(2)}, u32[]{:S(2)}) collective-permute-start(f16[48,512]{1,0:T(8,128)(2,1)S(1)} %multiply_convert_fusion), channel_id=1, source_target_pairs={{0,3},{1,2},{2,1},{3,0},{4,7},{5,6},{6,5},{7,4},{8,11},{9,10},{10,... | collective-permute-start | bytes 147464 | tf_op jit(solution)/shard_map/ppermute | solution.py:284
  11.2 3.2 %collective-permute-start.2 = (f16[48,512]{1,0:T(8,128)(2,1)S(1)}, f16[48,512]{1,0:T(8,128)(2,1)S(1)}, u32[]{:S(2)}, u32[]{:S(2)}) collective-permute-start(f16[48,512]{1,0:T(8,128)(2,1)S(1)} %multiply_convert_fusion), channel_id=1, source_target_pairs={{0,1},{1,0},{2,3},{3,2},{4,5},{5,4},{6,7},{7,6},{8,9},{9,8},{10,11... | collective-permute-start | bytes 147464 | tf_op jit(solution)/shard_map/ppermute | solution.py:292
  14.5 1.5 %collective-permute-start.6 = (bf16[48,128]{1,0:T(8,128)(2,1)S(1)}, bf16[48,128]{1,0:T(8,128)(2,1)S(1)}, u32[]{:S(2)}, u32[]{:S(2)}) collective-permute-start(bf16[48,128]{1,0:T(8,128)(2,1)S(1)} %fusion), channel_id=1, source_target_pairs={{0,1},{1,0},{2,3},{3,2},{4,5},{5,4},{6,7},{7,6},{8,9},{9,8},{10,11... | collective-permute-start | bytes 36872 | tf_op jit(solution)/shard_map/ppermute | solution.py:314

commit v6 on v5

--- a/solution.py
+++ b/solution.py
@@ -276,8 +276,9 @@
     count, cores = lax.axis_size("space"), lax.axis_size("tm")
     others = []
     for mask in masks:
+        mask = mask if isinstance(mask, tuple) else (mask, mask)
         pairs = [
-            (place * cores + core, (place ^ mask) * cores + (core ^ swap))
+            (place * cores + core, (place ^ mask[place >> 1 & 1]) * cores + (core ^ swap))
             for place in range(count)
             for core in range(cores)
         ]
@@ -289,9 +290,7 @@
     message = (values * scale).astype(jnp.float16)
     if ready is not None:
         message, ready = lax.optimization_barrier((message, ready))
-    others = [lax.ppermute(message, "tm", [(0, 1), (1, 0)])] if swap else []
-    others += received(message, masks, swap)
-    more = sum(other.astype(jnp.float32) for other in others) * (1 / scale)
+    more = sum(other.astype(jnp.float32) for other in received(message, masks, swap)) * (1 / scale)
     values = more if swap else values + more
     return values if ready is None else (values, ready)
 
@@ -301,7 +300,7 @@
     devices = lax.axis_size("space")
     dofs = columns.shape[1]
     coeffs = coefficients(columns, snapshots)
-    coeffs = exchanged(coeffs, (4,), message_scale(dofs, dofs * devices), 1)
+    coeffs = exchanged(coeffs, ((0, 4), (4, 0)), message_scale(dofs, dofs * devices), 1)
     gain = jnp.broadcast_to(mode_gain[:, None], (mode_gain.shape[0], HALF))
     taps, gain = lax.optimization_barrier((padded_taps(filter_taps), gain))
     bands = band_matrices(taps)
@@ -309,7 +308,7 @@
     while apart < devices:
         coeffs = exchanged(coeffs, (apart,), message_scale(dofs * apart // 4, dofs * devices), 0)
         apart *= 2
-    coeffs, bands = exchanged(coeffs, (1, 2, 3), message_scale(dofs * devices // 4, dofs * devices), 1, bands)
+    coeffs, bands = exchanged(coeffs, (0, 1, 2, 3), message_scale(dofs * devices // 4, dofs * devices), 1, bands)
     edge = jnp.where(lax.axis_index("tm") == 0, coeffs[:, -HALF:], coeffs[:, :HALF])
     halo = lax.ppermute(edge.astype(jnp.bfloat16), "tm", [(0, 1), (1, 0)])
     return band_field(coeffs, halo, [bands], gain, columns)

time: 17.4 us -> 17.4 us (level)
    ppermute x2 -> x0, starting transfers between devices: 0.22 us -> none  [exchanged(): others = [lax.ppermute(message, 'tm', [(0, 1), (1, 0)])] if swap else []]
    ppermute x4 -> x6, starting transfers between devices: 3.99 us -> 4.15 us  [received(): others.append(lax.ppermute(message, ('space', 'tm'), pairs))]
    ppermute x4 -> x6, waiting for transfers between devices: 6.61 us -> 6.61 us  [received(): others.append(lax.ppermute(message, ('space', 'tm'), pairs))]
where the time goes in v6:
time: 17.4 us; the launch traced here: 17.1 us
  waiting for transfers between devices  6.61 us (38%)
  starting transfers between devices  4.61 us (26%)
  Pallas kernels  4.31 us (25%)
  local copies, waits for them, and re-layouts  1.46 us (8%)
    ppermute x6, waiting for transfers between devices, received(): others.append(lax.ppermute(message, ('space', 'tm'), pairs))  6.61 us
    ppermute x6, starting transfers between devices, received(): others.append(lax.ppermute(message, ('space', 'tm'), pairs))  4.15 us
    pallas_call x1, Pallas kernels, coefficients(): pl.pallas_call(coefficient_kernel, out_shape=pltpu.VMEM((rows, steps), jn...  1.61 us
    pallas_call x1, Pallas kernels, band_field(): pl.pallas_call(functools.partial(edge_kernel, chunks, parts), grid=grid,...  1.21 us
    pallas_call x1, Pallas kernels, band_field(): pl.pallas_call(functools.partial(own_kernel, chunks, parts), grid=grid, o...  1.01 us
    reshape x1, local copies, waits for them, and re-layouts, padded_taps(): rows = filter_taps.astype(jnp.float32).reshape(freqs * parts, taps)  0.73 us
    broadcast_in_dim x1, local copies, waits for them, and re-layouts, per_device(): gain = jnp.broadcast_to(mode_gain[:, None], (mode_gain.shape[0], HALF))  0.73 us
    pallas_call x1, Pallas kernels, band_matrices(): pl.pallas_call(band_kernel, grid=() if one else (freqs // chunk,), out_sh...  0.47 us
  transfers between devices with their start and end apart: 7, of which 4 were waited for; matrix products, arithmetic and copies ran while one was open for 9% of the time, Pallas kernels for 9%

profile of v6, /device:TPU:25, one launch (start us, length us, event | category | flops | bytes accessed | tf_op | source)
XLA Modules:
  0.0 17.1 jit_solution(159816725191409113)
XLA Ops:
  0.0 0.0 copy-start
  0.0 1.6 %coefficients.1 = f32[48,512]{1,0:T(8,128)S(1)} custom-call(bf16[48,1024]{1,0:T(8,128)(2,1)} %bitcast.1, bf16[512,1024]{1,0:T(8,128)(2,1)} %snapshots_hbm.1), custom_call_target="tpu_custom_call" | custom-call | flops 50331648 | bytes 1048576 | tf_op jit(solution)/shard_map/coefficients/pallas_call | solution.py:42
  1.6 0.7 %collective-permute-start.1 = (f16[48,512]{1,0:T(8,128)(2,1)S(1)}, f16[48,512]{1,0:T(8,128)(2,1)S(1)}, u32[]{:S(2)}, u32[]{:S(2)}) collective-permute-start(f16[48,512]{1,0:T(8,128)(2,1)S(1)} %multiply_convert_fusion.1), channel_id=1, source_target_pairs={{0,9},{1,8},{2,11},{3,10},{4,5},{5,4},{6,7},{7,6},{8,1},{9,0},{10,... | collective-permute-start | bytes 147464 | tf_op jit(solution)/shard_map/ppermute | solution.py:285
  2.4 0.0 collective-permute-start
  2.4 0.7 %reshape.5 = bf16[16,257]{1,0:T(8,128)(2,1)S(1)} reshape(bf16[8,2,257]{2,1,0:T(2,128)(2,1)} %param.6) | data formatting | bytes 16448 | tf_op jit(solution)/shard_map/reshape | solution.py:72
  3.1 0.7 %broadcast_in_dim.2.refs_1_ = f32[48,128]{1,0:T(8,128)S(1)} broadcast(f32[48]{0:T(128)} %param.7), dimensions={0} | broadcast | bytes 24768 | tf_op jit(solution)/shard_map/broadcast_in_dim | solution.py:304
  3.9 0.5 %band_matrices.1.refs_0_ = bf16[8,128,768]{2,1,0:T(8,128)(2,1)S(1)} custom-call(f32[16,384]{1,0:T(8,128)S(1)} %pad_convert_fusion.taps_ref), custom_call_target="tpu_custom_call" | custom-call | flops 15728640 | bytes 1572864 | tf_op jit(solution)/shard_map/band_matrices/pallas_call | solution.py:81
  4.4 0.0 collective-permute-done.1
  4.4 3.4 %collective-permute-done = f16[48,512]{1,0:T(8,128)(2,1)S(1)} collective-permute-done((f16[48,512]{1,0:T(8,128)(2,1)S(1)}, f16[48,512]{1,0:T(8,128)(2,1)S(1)}, u32[]{:S(2)}, u32[]{:S(2)}) %collective-permute-start) | collective-permute-done | bytes 49184 | tf_op jit(solution)/shard_map/ppermute | solution.py:285
  7.8 0.6 %collective-permute-start.5 = (f16[48,512]{1,0:T(8,128)(2,1)S(1)}, f16[48,512]{1,0:T(8,128)(2,1)S(1)}, u32[]{:S(2)}, u32[]{:S(2)}) collective-permute-start(f16[48,512]{1,0:T(8,128)(2,1)S(1)} %multiply_convert_fusion), channel_id=1, source_target_pairs={{0,7},{1,6},{2,5},{3,4},{4,3},{5,2},{6,1},{7,0},{8,15},{9,14},{10,... | collective-permute-start | bytes 147464 | tf_op jit(solution)/shard_map/ppermute | solution.py:285
  8.5 2.1 %collective-permute-start.4 = (f16[48,512]{1,0:T(8,128)(2,1)S(1)}, f16[48,512]{1,0:T(8,128)(2,1)S(1)}, u32[]{:S(2)}, u32[]{:S(2)}) collective-permute-start(f16[48,512]{1,0:T(8,128)(2,1)S(1)} %multiply_convert_fusion), channel_id=1, source_target_pairs={{0,5},{1,4},{2,7},{3,6},{4,1},{5,0},{6,3},{7,2},{8,13},{9,12},{10,... | collective-permute-start | bytes 147464 | tf_op jit(solution)/shard_map/ppermute | solution.py:285
  10.6 0.6 %collective-permute-start.3 = (f16[48,512]{1,0:T(8,128)(2,1)S(1)}, f16[48,512]{1,0:T(8,128)(2,1)S(1)}, u32[]{:S(2)}, u32[]{:S(2)}) collective-permute-start(f16[48,512]{1,0:T(8,128)(2,1)S(1)} %multiply_convert_fusion), channel_id=1, source_target_pairs={{0,3},{1,2},{2,1},{3,0},{4,7},{5,6},{6,5},{7,4},{8,11},{9,10},{10,... | collective-permute-start | bytes 147464 | tf_op jit(solution)/shard_map/ppermute | solution.py:285
  11.1 0.1 collective-permute-start.2
  11.2 1.6 %collective-permute-done.5 = f16[48,512]{1,0:T(8,128)(2,1)S(1)} collective-permute-done((f16[48,512]{1,0:T(8,128)(2,1)S(1)}, f16[48,512]{1,0:T(8,128)(2,1)S(1)}, u32[]{:S(2)}, u32[]{:S(2)}) %collective-permute-start.5) | collective-permute-done | bytes 49184 | tf_op jit(solution)/shard_map/ppermute | solution.py:285
  12.8 1.1 %collective-permute-done.4 = f16[48,512]{1,0:T(8,128)(2,1)S(1)} collective-permute-done((f16[48,512]{1,0:T(8,128)(2,1)S(1)}, f16[48,512]{1,0:T(8,128)(2,1)S(1)}, u32[]{:S(2)}, u32[]{:S(2)}) %collective-permute-start.4) | collective-permute-done | bytes 49184 | tf_op jit(solution)/shard_map/ppermute | solution.py:285
  13.9 0.5 %collective-permute-done.3 = f16[48,512]{1,0:T(8,128)(2,1)S(1)} collective-permute-done((f16[48,512]{1,0:T(8,128)(2,1)S(1)}, f16[48,512]{1,0:T(8,128)(2,1)S(1)}, u32[]{:S(2)}, u32[]{:S(2)}) %collective-permute-start.3) | collective-permute-done | bytes 49184 | tf_op jit(solution)/shard_map/ppermute | solution.py:285
  14.4 0.0 collective-permute-done.2
  14.4 0.5 %collective-permute-start.6 = (bf16[48,128]{1,0:T(8,128)(2,1)S(1)}, bf16[48,128]{1,0:T(8,128)(2,1)S(1)}, u32[]{:S(2)}, u32[]{:S(2)}) collective-permute-start(bf16[48,128]{1,0:T(8,128)(2,1)S(1)} %fusion), channel_id=1, source_target_pairs={{0,1},{1,0},{2,3},{3,2},{4,5},{5,4},{6,7},{7,6},{8,9},{9,8},{10,11... | collective-permute-start | bytes 36872 | tf_op jit(solution)/shard_map/ppermute | solution.py:313
  14.9 0.0 copy-done
  14.9 1.0 %own_field.1 = (f32[48,512]{1,0:T(8,128)S(1)}, bf16[512,1024]{1,0:T(8,128)(2,1)S(1)}) custom-call(f32[48,512]{1,0:T(8,128)S(1)} %add_multiply_fusion.coeffs_ref, bf16[8,128,768]{2,1,0:T(8,128)(2,1)S(1)} %band_matrices.1.refs_0_, f32[48,128]{1,0:T(8,128)S(1)} %broadcast_in_dim.2.refs_1_, bf16[48,1024]{1,0:T(8,128)(2,1)S(1)} %bitcast.2), custom_call_target="tpu_custom_call" | custom-call | flops 50331648 | bytes 1048576 | tf_op jit(solution)/shard_map/own_field/pallas_call | solution.py:233
  15.9 0.0 collective-permute-done.6.halo_ref
  15.9 1.2 %edge_field.1 = bf16[512,1024]{1,0:T(8,128)(2,1)} custom-call(bf16[48,128]{1,0:T(8,128)(2,1)S(1)} %collective-permute-done.6.halo_ref, f32[48,512]{1,0:T(8,128)S(1)} %get-tuple-element.15.filtered_ref, bf16[8,128,768]{2,1,0:T(8,128)(2,1)S(1)} %band_matrices.1.refs_0_, f32[48,128]{1,0:T(8,128)S(1)} %broadcast_in_dim.2.refs_1_, bf16[48,1024]{1,0:T(8,128)(2,1)S(1)} %bitcast.3, ...), custom_call_target="tpu_custom_call" | custom-call | flops 12582912 | bytes 1048576 | tf_op jit(solution)/shard_map/edge_field/pallas_call | solution.py:249
  (5 shorter events, 0.1 us)
Async XLA Ops:
  0.0 14.9 %copy-start = (bf16[1024,48]{0,1:T(8,128)(2,1)S(1)}, bf16[1024,48]{0,1:T(8,128)(2,1)}, u32[]{:S(2)}) copy-start(bf16[1024,48]{0,1:T(8,128)(2,1)} %param.5) | copy-start | bytes 294916
  1.6 2.7 %collective-permute-start.1 = (f16[48,512]{1,0:T(8,128)(2,1)S(1)}, f16[48,512]{1,0:T(8,128)(2,1)S(1)}, u32[]{:S(2)}, u32[]{:S(2)}) collective-permute-start(f16[48,512]{1,0:T(8,128)(2,1)S(1)} %multiply_convert_fusion.1), channel_id=1, source_target_pairs={{0,9},{1,8},{2,11},{3,10},{4,5},{5,4},{6,7},{7,6},{8,1},{9,0},{10,... | collective-permute-start | bytes 147464 | tf_op jit(solution)/shard_map/ppermute | solution.py:285
  2.4 5.4 %collective-permute-start = (f16[48,512]{1,0:T(8,128)(2,1)S(1)}, f16[48,512]{1,0:T(8,128)(2,1)S(1)}, u32[]{:S(2)}, u32[]{:S(2)}) collective-permute-start(f16[48,512]{1,0:T(8,128)(2,1)S(1)} %multiply_convert_fusion.1), channel_id=1, source_target_pairs={{0,1},{1,0},{2,3},{3,2},{4,13},{5,12},{6,15},{7,14},{8,9},{9,8},{1... | collective-permute-start | bytes 147464 | tf_op jit(solution)/shard_map/ppermute | solution.py:285
  7.8 5.0 %collective-permute-start.5 = (f16[48,512]{1,0:T(8,128)(2,1)S(1)}, f16[48,512]{1,0:T(8,128)(2,1)S(1)}, u32[]{:S(2)}, u32[]{:S(2)}) collective-permute-start(f16[48,512]{1,0:T(8,128)(2,1)S(1)} %multiply_convert_fusion), channel_id=1, source_target_pairs={{0,7},{1,6},{2,5},{3,4},{4,3},{5,2},{6,1},{7,0},{8,15},{9,14},{10,... | collective-permute-start | bytes 147464 | tf_op jit(solution)/shard_map/ppermute | solution.py:285
  8.5 5.4 %collective-permute-start.4 = (f16[48,512]{1,0:T(8,128)(2,1)S(1)}, f16[48,512]{1,0:T(8,128)(2,1)S(1)}, u32[]{:S(2)}, u32[]{:S(2)}) collective-permute-start(f16[48,512]{1,0:T(8,128)(2,1)S(1)} %multiply_convert_fusion), channel_id=1, source_target_pairs={{0,5},{1,4},{2,7},{3,6},{4,1},{5,0},{6,3},{7,2},{8,13},{9,12},{10,... | collective-permute-start | bytes 147464 | tf_op jit(solution)/shard_map/ppermute | solution.py:285
  10.6 3.8 %collective-permute-start.3 = (f16[48,512]{1,0:T(8,128)(2,1)S(1)}, f16[48,512]{1,0:T(8,128)(2,1)S(1)}, u32[]{:S(2)}, u32[]{:S(2)}) collective-permute-start(f16[48,512]{1,0:T(8,128)(2,1)S(1)} %multiply_convert_fusion), channel_id=1, source_target_pairs={{0,3},{1,2},{2,1},{3,0},{4,7},{5,6},{6,5},{7,4},{8,11},{9,10},{10,... | collective-permute-start | bytes 147464 | tf_op jit(solution)/shard_map/ppermute | solution.py:285
  11.1 3.2 %collective-permute-start.2 = (f16[48,512]{1,0:T(8,128)(2,1)S(1)}, f16[48,512]{1,0:T(8,128)(2,1)S(1)}, u32[]{:S(2)}, u32[]{:S(2)}) collective-permute-start(f16[48,512]{1,0:T(8,128)(2,1)S(1)} %multiply_convert_fusion), channel_id=1, source_target_pairs={{0,1},{1,0},{2,3},{3,2},{4,5},{5,4},{6,7},{7,6},{8,9},{9,8},{10,11... | collective-permute-start | bytes 147464 | tf_op jit(solution)/shard_map/ppermute | solution.py:285
  14.4 1.5 %collective-permute-start.6 = (bf16[48,128]{1,0:T(8,128)(2,1)S(1)}, bf16[48,128]{1,0:T(8,128)(2,1)S(1)}, u32[]{:S(2)}, u32[]{:S(2)}) collective-permute-start(bf16[48,128]{1,0:T(8,128)(2,1)S(1)} %fusion), channel_id=1, source_target_pairs={{0,1},{1,0},{2,3},{3,2},{4,5},{5,4},{6,7},{7,6},{8,9},{9,8},{10,11... | collective-permute-start | bytes 36872 | tf_op jit(solution)/shard_map/ppermute | solution.py:313

commit v7 on v6

--- a/solution.py
+++ b/solution.py
@@ -122,37 +122,47 @@
     each = bands[0].shape[0]
     freqs = parts * each
     modes = rows // freqs
+    half = HALF // 2
     cells = coeffs_ref[...].astype(jnp.bfloat16).astype(jnp.float32)
+    none = jnp.zeros((rows, HALF), jnp.float32)
+    cells = jnp.concatenate([none, cells, none], axis=1)
+    extent = cells.shape[1]
     for i, part in enumerate((cells, turned(cells))):
-        wide[i, :, :HALF] = jnp.zeros((rows + 8, HALF), jnp.float32)
-        wide[i, :, HALF + steps :] = jnp.zeros((rows + 8, HALF), jnp.float32)
-        wide[i, :rows, HALF : HALF + steps] = part
-        wide[i, rows:, HALF : HALF + steps] = jnp.zeros((8, steps), jnp.float32)
+        wide[i, :rows, :] = part
+        wide[2 + i, :rows, :] = pltpu.roll(part, extent - half, 1)
+    wide[:, rows:, :] = jnp.zeros((4, 8, extent), jnp.float32)
     for f in range(freqs):
         at = f * modes
-        both = [wide[i, at : at + 8, :] for i in range(2)]
         inputs = jnp.concatenate(
             [
-                jnp.concatenate([part[:, b * HALF : b * HALF + WINDOW] for part in both], axis=1)
+                jnp.concatenate(
+                    [wide[2 * late + i, at : at + 8, b * HALF : b * HALF + WINDOW] for i in range(2)], axis=1
+                )
                 for b in range(blocks)
+                for late in range(2)
             ],
             axis=0,
         ).astype(jnp.bfloat16)
-        band = bands[f // each][f % each]
+        band = bands[f // each][f % each, :half, :]
         filtered = lax.dot_general(inputs, band, LAST, preferred_element_type=jnp.float32)
         for b in range(blocks):
-            filtered_ref[at : at + modes, b * HALF : (b + 1) * HALF] = filtered[8 * b : 8 * b + modes]
+            pair = [filtered[8 * k : 8 * k + modes] for k in (2 * b, 2 * b + 1)]
+            filtered_ref[at : at + modes, b * HALF : (b + 1) * HALF] = jnp.concatenate(pair, axis=1)
     columns = columns_ref[...]
     rest, _ = places(steps)
-    for b in range(blocks - 1):
-        span = pl.ds(pl.multiple_of(rest + b * HALF, HALF), HALF)
-        piece = (filtered_ref[:, span] * gain_ref[...]).astype(jnp.bfloat16)
-        part = lax.dot_general(piece, columns, FIRST, preferred_element_type=jnp.float32)
-
-        def store(values, span=span):
-            field_ref[span, :] = values.astype(jnp.bfloat16)
-
-        add_over_chunks(chunks, total, (span, slice(None)), part, store)
+    alone = steps - HALF
+    span = pl.ds(rest, alone)
+    gain = jnp.concatenate([gain_ref[...]] * (blocks - 1), axis=1)
+    piece = (filtered_ref[:, span] * gain).astype(jnp.bfloat16)
+    width = columns.shape[1] // SPLITS
+    for i in range(SPLITS):
+        place = (span, slice(i * width, (i + 1) * width))
+        part = lax.dot_general(piece, columns[:, place[1]], FIRST, preferred_element_type=jnp.float32)
+
+        def store(values, place=place):
+            field_ref[place] = values.astype(jnp.bfloat16)
+
+        add_over_chunks(chunks, total, place, part, store)
 
 
 def edge_kernel(chunks, parts, halo_ref, filtered_ref, *refs):
@@ -237,7 +247,7 @@
         in_specs=[rows_of(steps), *taps, rows_of(HALF), rows_of(dofs)],
         out_specs=[rows_of(steps), WHOLE],
         scratch_shapes=[
-            pltpu.VMEM((2, held + 8, steps + 2 * HALF), jnp.float32),
+            pltpu.VMEM((4, held + 8, steps + 2 * HALF), jnp.float32),
             pltpu.VMEM((8 if one else steps, dofs), jnp.float32),
         ],
         compiler_params=params,
@@ -290,9 +300,14 @@
     message = (values * scale).astype(jnp.float16)
     if ready is not None:
         message, ready = lax.optimization_barrier((message, ready))
-    more = sum(other.astype(jnp.float32) for other in received(message, masks, swap)) * (1 / scale)
-    values = more if swap else values + more
-    return values if ready is None else (values, ready)
+    others = received(message, masks, swap)
+    more = sum(other.astype(jnp.float32) for other in others) * (1 / scale)
+    if ready is None:
+        return more if swap else values + more
+    low = lax.axis_index("tm") == 0
+    ends = [jnp.where(low, other[:, -HALF:], other[:, :HALF]).astype(jnp.float32) for other in others]
+    edge = (sum(ends) * (1 / scale)).astype(jnp.bfloat16)
+    return more, edge, ready
 
 
 def per_device(snapshots, mode_columns, filter_taps, mode_gain):
@@ -308,9 +323,8 @@
     while apart < devices:
         coeffs = exchanged(coeffs, (apart,), message_scale(dofs * apart // 4, dofs * devices), 0)
         apart *= 2
-    coeffs, bands = exchanged(coeffs, (0, 1, 2, 3), message_scale(dofs * devices // 4, dofs * devices), 1, bands)
-    edge = jnp.where(lax.axis_index("tm") == 0, coeffs[:, -HALF:], coeffs[:, :HALF])
-    halo = lax.ppermute(edge.astype(jnp.bfloat16), "tm", [(0, 1), (1, 0)])
+    coeffs, edge, bands = exchanged(coeffs, (0, 1, 2, 3), message_scale(dofs * devices // 4, dofs * devices), 1, bands)
+    halo = lax.ppermute(edge, "tm", [(0, 1), (1, 0)])
     return band_field(coeffs, halo, [bands], gain, columns)
 
 

time: 17.4 us -> 17.3 us (level)
  transfers between devices with their start and end apart: 7 -> 7, of which waited for: 4 -> 4; matrix products, arithmetic and copies ran while one was open for 9% -> 9% of each run, Pallas kernels for 9% -> 8%
where the time goes in v7:
time: 17.3 us; the launch traced here: 17 us
  waiting for transfers between devices  6.61 us (38%)
  starting transfers between devices  4.61 us (27%)
  Pallas kernels  4.19 us (24%)
  local copies, waits for them, and re-layouts  1.46 us (8%)
    ppermute x6, waiting for transfers between devices, received(): others.append(lax.ppermute(message, ('space', 'tm'), pairs))  6.61 us
    ppermute x6, starting transfers between devices, received(): others.append(lax.ppermute(message, ('space', 'tm'), pairs))  4.15 us
    pallas_call x1, Pallas kernels, coefficients(): pl.pallas_call(coefficient_kernel, out_shape=pltpu.VMEM((rows, steps), jn...  1.61 us
    pallas_call x1, Pallas kernels, band_field(): pl.pallas_call(functools.partial(edge_kernel, chunks, parts), grid=grid,...  1.22 us
    pallas_call x1, Pallas kernels, band_field(): pl.pallas_call(functools.partial(own_kernel, chunks, parts), grid=grid, o...  0.89 us
    reshape x1, local copies, waits for them, and re-layouts, padded_taps(): rows = filter_taps.astype(jnp.float32).reshape(freqs * parts, taps)  0.73 us
    broadcast_in_dim x1, local copies, waits for them, and re-layouts, per_device(): gain = jnp.broadcast_to(mode_gain[:, None], (mode_gain.shape[0], HALF))  0.73 us
    pallas_call x1, Pallas kernels, band_matrices(): pl.pallas_call(band_kernel, grid=() if one else (freqs // chunk,), out_sh...  0.47 us
  transfers between devices with their start and end apart: 7, of which 4 were waited for; matrix products, arithmetic and copies ran while one was open for 9% of the time, Pallas kernels for 8%

profile of v7, /device:TPU:25, one launch (start us, length us, event | category | flops | bytes accessed | tf_op | source)
XLA Modules:
  0.0 17.0 jit_solution(5828996925834681727)
XLA Ops:
  0.0 0.0 copy-start
  0.0 1.6 %coefficients.1 = f32[48,512]{1,0:T(8,128)S(1)} custom-call(bf16[48,1024]{1,0:T(8,128)(2,1)} %bitcast.1, bf16[512,1024]{1,0:T(8,128)(2,1)} %snapshots_hbm.1), custom_call_target="tpu_custom_call" | custom-call | flops 50331648 | bytes 1048576 | tf_op jit(solution)/shard_map/coefficients/pallas_call | solution.py:42
  1.6 0.7 %collective-permute-start.1 = (f16[48,512]{1,0:T(8,128)(2,1)S(1)}, f16[48,512]{1,0:T(8,128)(2,1)S(1)}, u32[]{:S(2)}, u32[]{:S(2)}) collective-permute-start(f16[48,512]{1,0:T(8,128)(2,1)S(1)} %multiply_convert_fusion.1), channel_id=1, source_target_pairs={{0,9},{1,8},{2,11},{3,10},{4,5},{5,4},{6,7},{7,6},{8,1},{9,0},{10,... | collective-permute-start | bytes 147464 | tf_op jit(solution)/shard_map/ppermute | solution.py:295
  2.4 0.0 collective-permute-start
  2.4 0.7 %reshape.5 = bf16[16,257]{1,0:T(8,128)(2,1)S(1)} reshape(bf16[8,2,257]{2,1,0:T(2,128)(2,1)} %param.6) | data formatting | bytes 16448 | tf_op jit(solution)/shard_map/reshape | solution.py:72
  3.1 0.7 %broadcast_in_dim.2.refs_1_ = f32[48,128]{1,0:T(8,128)S(1)} broadcast(f32[48]{0:T(128)} %param.7), dimensions={0} | broadcast | bytes 24768 | tf_op jit(solution)/shard_map/broadcast_in_dim | solution.py:319
  3.9 0.5 %band_matrices.1.refs_0_ = bf16[8,128,768]{2,1,0:T(8,128)(2,1)S(1)} custom-call(f32[16,384]{1,0:T(8,128)S(1)} %pad_convert_fusion.taps_ref), custom_call_target="tpu_custom_call" | custom-call | flops 15728640 | bytes 1572864 | tf_op jit(solution)/shard_map/band_matrices/pallas_call | solution.py:81
  4.4 0.0 collective-permute-done.1
  4.4 3.4 %collective-permute-done = f16[48,512]{1,0:T(8,128)(2,1)S(1)} collective-permute-done((f16[48,512]{1,0:T(8,128)(2,1)S(1)}, f16[48,512]{1,0:T(8,128)(2,1)S(1)}, u32[]{:S(2)}, u32[]{:S(2)}) %collective-permute-start) | collective-permute-done | bytes 49184 | tf_op jit(solution)/shard_map/ppermute | solution.py:295
  7.8 0.6 %collective-permute-start.5 = (f16[48,512]{1,0:T(8,128)(2,1)S(1)}, f16[48,512]{1,0:T(8,128)(2,1)S(1)}, u32[]{:S(2)}, u32[]{:S(2)}) collective-permute-start(f16[48,512]{1,0:T(8,128)(2,1)S(1)} %multiply_convert_fusion), channel_id=1, source_target_pairs={{0,7},{1,6},{2,5},{3,4},{4,3},{5,2},{6,1},{7,0},{8,15},{9,14},{10,... | collective-permute-start | bytes 147464 | tf_op jit(solution)/shard_map/ppermute | solution.py:295
  8.5 2.1 %collective-permute-start.4 = (f16[48,512]{1,0:T(8,128)(2,1)S(1)}, f16[48,512]{1,0:T(8,128)(2,1)S(1)}, u32[]{:S(2)}, u32[]{:S(2)}) collective-permute-start(f16[48,512]{1,0:T(8,128)(2,1)S(1)} %multiply_convert_fusion), channel_id=1, source_target_pairs={{0,5},{1,4},{2,7},{3,6},{4,1},{5,0},{6,3},{7,2},{8,13},{9,12},{10,... | collective-permute-start | bytes 147464 | tf_op jit(solution)/shard_map/ppermute | solution.py:295
  10.6 0.6 %collective-permute-start.3 = (f16[48,512]{1,0:T(8,128)(2,1)S(1)}, f16[48,512]{1,0:T(8,128)(2,1)S(1)}, u32[]{:S(2)}, u32[]{:S(2)}) collective-permute-start(f16[48,512]{1,0:T(8,128)(2,1)S(1)} %multiply_convert_fusion), channel_id=1, source_target_pairs={{0,3},{1,2},{2,1},{3,0},{4,7},{5,6},{6,5},{7,4},{8,11},{9,10},{10,... | collective-permute-start | bytes 147464 | tf_op jit(solution)/shard_map/ppermute | solution.py:295
  11.1 0.1 collective-permute-start.2
  11.2 1.6 %collective-permute-done.5 = f16[48,512]{1,0:T(8,128)(2,1)S(1)} collective-permute-done((f16[48,512]{1,0:T(8,128)(2,1)S(1)}, f16[48,512]{1,0:T(8,128)(2,1)S(1)}, u32[]{:S(2)}, u32[]{:S(2)}) %collective-permute-start.5) | collective-permute-done | bytes 49184 | tf_op jit(solution)/shard_map/ppermute | solution.py:295
  12.8 1.1 %collective-permute-done.4 = f16[48,512]{1,0:T(8,128)(2,1)S(1)} collective-permute-done((f16[48,512]{1,0:T(8,128)(2,1)S(1)}, f16[48,512]{1,0:T(8,128)(2,1)S(1)}, u32[]{:S(2)}, u32[]{:S(2)}) %collective-permute-start.4) | collective-permute-done | bytes 49184 | tf_op jit(solution)/shard_map/ppermute | solution.py:295
  13.9 0.5 %collective-permute-done.3 = f16[48,512]{1,0:T(8,128)(2,1)S(1)} collective-permute-done((f16[48,512]{1,0:T(8,128)(2,1)S(1)}, f16[48,512]{1,0:T(8,128)(2,1)S(1)}, u32[]{:S(2)}, u32[]{:S(2)}) %collective-permute-start.3) | collective-permute-done | bytes 49184 | tf_op jit(solution)/shard_map/ppermute | solution.py:295
  14.4 0.0 collective-permute-done.2
  14.4 0.5 %collective-permute-start.6 = (bf16[48,128]{1,0:T(8,128)(2,1)S(1)}, bf16[48,128]{1,0:T(8,128)(2,1)S(1)}, u32[]{:S(2)}, u32[]{:S(2)}) collective-permute-start(bf16[48,128]{1,0:T(8,128)(2,1)S(1)} %multiply_convert_fusion.2), channel_id=1, source_target_pairs={{0,1},{1,0},{2,3},{3,2},{4,5},{5,4},{6,7},{7,6},{8,9},{9,8},{10,11... | collective-permute-start | bytes 36872 | tf_op jit(solution)/shard_map/ppermute | solution.py:327
  14.9 0.0 copy-done
  14.9 0.9 %own_field.1 = (f32[48,512]{1,0:T(8,128)S(1)}, bf16[512,1024]{1,0:T(8,128)(2,1)S(1)}) custom-call(f32[48,512]{1,0:T(8,128)S(1)} %add_multiply_fusion.coeffs_ref, bf16[8,128,768]{2,1,0:T(8,128)(2,1)S(1)} %band_matrices.1.refs_0_, f32[48,128]{1,0:T(8,128)S(1)} %broadcast_in_dim.2.refs_1_, bf16[48,1024]{1,0:T(8,128)(2,1)S(1)} %bitcast.2), custom_call_target="tpu_custom_call" | custom-call | flops 50331648 | bytes 1048576 | tf_op jit(solution)/shard_map/own_field/pallas_call | solution.py:243
  15.8 0.0 collective-permute-done.6.halo_ref
  15.8 1.2 %edge_field.1 = bf16[512,1024]{1,0:T(8,128)(2,1)} custom-call(bf16[48,128]{1,0:T(8,128)(2,1)S(1)} %collective-permute-done.6.halo_ref, f32[48,512]{1,0:T(8,128)S(1)} %get-tuple-element.15.filtered_ref, bf16[8,128,768]{2,1,0:T(8,128)(2,1)S(1)} %band_matrices.1.refs_0_, f32[48,128]{1,0:T(8,128)S(1)} %broadcast_in_dim.2.refs_1_, bf16[48,1024]{1,0:T(8,128)(2,1)S(1)} %bitcast.3, ...), custom_call_target="tpu_custom_call" | custom-call | flops 12582912 | bytes 1048576 | tf_op jit(solution)/shard_map/edge_field/pallas_call | solution.py:259
  (5 shorter events, 0.1 us)
Async XLA Ops:
  0.0 14.9 %copy-start = (bf16[1024,48]{0,1:T(8,128)(2,1)S(1)}, bf16[1024,48]{0,1:T(8,128)(2,1)}, u32[]{:S(2)}) copy-start(bf16[1024,48]{0,1:T(8,128)(2,1)} %param.5) | copy-start | bytes 294916
  1.6 2.7 %collective-permute-start.1 = (f16[48,512]{1,0:T(8,128)(2,1)S(1)}, f16[48,512]{1,0:T(8,128)(2,1)S(1)}, u32[]{:S(2)}, u32[]{:S(2)}) collective-permute-start(f16[48,512]{1,0:T(8,128)(2,1)S(1)} %multiply_convert_fusion.1), channel_id=1, source_target_pairs={{0,9},{1,8},{2,11},{3,10},{4,5},{5,4},{6,7},{7,6},{8,1},{9,0},{10,... | collective-permute-start | bytes 147464 | tf_op jit(solution)/shard_map/ppermute | solution.py:295
  2.4 5.4 %collective-permute-start = (f16[48,512]{1,0:T(8,128)(2,1)S(1)}, f16[48,512]{1,0:T(8,128)(2,1)S(1)}, u32[]{:S(2)}, u32[]{:S(2)}) collective-permute-start(f16[48,512]{1,0:T(8,128)(2,1)S(1)} %multiply_convert_fusion.1), channel_id=1, source_target_pairs={{0,1},{1,0},{2,3},{3,2},{4,13},{5,12},{6,15},{7,14},{8,9},{9,8},{1... | collective-permute-start | bytes 147464 | tf_op jit(solution)/shard_map/ppermute | solution.py:295
  7.8 5.0 %collective-permute-start.5 = (f16[48,512]{1,0:T(8,128)(2,1)S(1)}, f16[48,512]{1,0:T(8,128)(2,1)S(1)}, u32[]{:S(2)}, u32[]{:S(2)}) collective-permute-start(f16[48,512]{1,0:T(8,128)(2,1)S(1)} %multiply_convert_fusion), channel_id=1, source_target_pairs={{0,7},{1,6},{2,5},{3,4},{4,3},{5,2},{6,1},{7,0},{8,15},{9,14},{10,... | collective-permute-start | bytes 147464 | tf_op jit(solution)/shard_map/ppermute | solution.py:295
  8.5 5.4 %collective-permute-start.4 = (f16[48,512]{1,0:T(8,128)(2,1)S(1)}, f16[48,512]{1,0:T(8,128)(2,1)S(1)}, u32[]{:S(2)}, u32[]{:S(2)}) collective-permute-start(f16[48,512]{1,0:T(8,128)(2,1)S(1)} %multiply_convert_fusion), channel_id=1, source_target_pairs={{0,5},{1,4},{2,7},{3,6},{4,1},{5,0},{6,3},{7,2},{8,13},{9,12},{10,... | collective-permute-start | bytes 147464 | tf_op jit(solution)/shard_map/ppermute | solution.py:295
  10.6 3.8 %collective-permute-start.3 = (f16[48,512]{1,0:T(8,128)(2,1)S(1)}, f16[48,512]{1,0:T(8,128)(2,1)S(1)}, u32[]{:S(2)}, u32[]{:S(2)}) collective-permute-start(f16[48,512]{1,0:T(8,128)(2,1)S(1)} %multiply_convert_fusion), channel_id=1, source_target_pairs={{0,3},{1,2},{2,1},{3,0},{4,7},{5,6},{6,5},{7,4},{8,11},{9,10},{10,... | collective-permute-start | bytes 147464 | tf_op jit(solution)/shard_map/ppermute | solution.py:295
  11.1 3.2 %collective-permute-start.2 = (f16[48,512]{1,0:T(8,128)(2,1)S(1)}, f16[48,512]{1,0:T(8,128)(2,1)S(1)}, u32[]{:S(2)}, u32[]{:S(2)}) collective-permute-start(f16[48,512]{1,0:T(8,128)(2,1)S(1)} %multiply_convert_fusion), channel_id=1, source_target_pairs={{0,1},{1,0},{2,3},{3,2},{4,5},{5,4},{6,7},{7,6},{8,9},{9,8},{10,11... | collective-permute-start | bytes 147464 | tf_op jit(solution)/shard_map/ppermute | solution.py:295
  14.4 1.4 %collective-permute-start.6 = (bf16[48,128]{1,0:T(8,128)(2,1)S(1)}, bf16[48,128]{1,0:T(8,128)(2,1)S(1)}, u32[]{:S(2)}, u32[]{:S(2)}) collective-permute-start(bf16[48,128]{1,0:T(8,128)(2,1)S(1)} %multiply_convert_fusion.2), channel_id=1, source_target_pairs={{0,1},{1,0},{2,3},{3,2},{4,5},{5,4},{6,7},{7,6},{8,9},{9,8},{10,11... | collective-permute-start | bytes 36872 | tf_op jit(solution)/shard_map/ppermute | solution.py:327
